TPU v7x, 128 devices: a whole 4x4x4 slice. The times are simulated.
128 devices in a mesh: dp: 16 (over x, z), ctx: 8 (over y, core).
Axes of the slice: x: 4, y: 4, z: 4, core: 2. Of those that a mesh axis runs over, the one named last changes fastest.
Arguments:
- tokens: bfloat16 [16, 1024, 896], P('dp', 'ctx'), may hold values from -6 to 6
- cotangent: bfloat16 [16, 1024, 896], P('dp', 'ctx'), may hold values from -6 to 6
- span_order: int32 [16], replicated, may hold values from 0 to 15, each once
- gain_one: bfloat16 [2, 896], P(None, ('dp', 'ctx')), may hold values from 0.5 to 1.5
- w_qkv: bfloat16 [2, 896, 1152], P(None, ('dp', 'ctx')), may hold values from -0.1875 to 0.1875
- b_qkv: bfloat16 [2, 1152], P(None, ('dp', 'ctx')), may hold values from -3 to 3
- w_out: bfloat16 [2, 896, 896], P(None, ('dp', 'ctx')), may hold values from -0.75 to 0.75
- gain_two: bfloat16 [2, 896], P(None, ('dp', 'ctx')), may hold values from 0.5 to 1.5
- w_gate: bfloat16 [2, 896, 4864], P(None, 'dp', 'ctx'), may hold values from -0.1875 to 0.1875
- w_up: bfloat16 [2, 896, 4864], P(None, 'dp', 'ctx'), may hold values from -0.1875 to 0.1875
- w_down: bfloat16 [2, 4864, 896], P(None, 'ctx', 'dp'), may hold values from -0.125 to 0.125
Outputs:
- result: bfloat16 [16, 1024, 896], P('dp', 'ctx')
- input_grad: float32 [16, 1024, 896], P('dp', 'ctx')
- grad_gain_one: float32 [2, 896], P(None, ('dp', 'ctx'))
- grad_w_qkv: float32 [2, 896, 1152], P(None, ('dp', 'ctx'))
- grad_b_qkv: float32 [2, 1024], P(None, ('dp', 'ctx'))
- grad_b_value: float32 [2, 128], P(None, ('dp', 'ctx'))
- grad_w_out: float32 [2, 896, 896], P(None, ('dp', 'ctx'))
- grad_gain_two: float32 [2, 896], P(None, ('dp', 'ctx'))
- grad_w_gate: float32 [2, 896, 4864], P(None, 'dp', 'ctx')
- grad_w_up: float32 [2, 896, 4864], P(None, 'dp', 'ctx')
- grad_w_down: float32 [2, 4864, 896], P(None, 'ctx', 'dp')
Inputs may be any that keep to these rules, and one draw needn't show every extreme that they name: Storage block j of every sequence (its tokens j * 64 to j * 64 + 63) holds the positions from span_order[j] * 64 on; span_order is a permutation.
All inputs are finite; a program needn't handle non-finite values.
Results may differ from a plain program's by a relative error of at most 0.04.
Values may be sent and summed in bfloat16 or wider, within the bound.
A program may use at most 192 MiB of HBM per device.

v0:
```python
import functools

import jax
import jax.numpy as jnp
import numpy as np
from jax import lax
from jax.experimental import pallas as pl
from jax.experimental.pallas import tpu as pltpu
from jax.sharding import PartitionSpec as P

H = 14
KVH = 2
HD = 64
LAYERS = 2
D = 896
QKV = 1152
FS = 608
MESH = pl.DeviceIdType.MESH
BF = jnp.bfloat16
F32 = jnp.float32

eps_norm = 1e-06
rope_base = 1000000.0
neg_fill = -1e30


def place():
    dp = lax.axis_index("dp")
    ctx = lax.axis_index("ctx")
    return lax.div(dp, 4), lax.rem(dp, 4), lax.div(ctx, 2), lax.rem(ctx, 2)


def up1(v):
    return lax.rem(v + 1, 4)


def up2(v):
    return lax.rem(v + 2, 4)


def down1(v):
    return lax.rem(v + 3, 4)


def device(x, z, y, c):
    return (x * 4 + z, y * 2 + c)


def greet(peers):
    barrier = pltpu.get_barrier_semaphore()
    for peer in peers:
        pl.semaphore_signal(barrier, inc=1, device_id=peer, device_id_type=MESH)
    pl.semaphore_wait(barrier, len(peers))


class Mail:
    def __init__(self, send_sem, recv_sem, base=0, sent=None):
        self.send_sem = send_sem
        self.recv_sem = recv_sem
        self.base = base
        self.sent = [] if sent is None else sent

    def shifted(self, base):
        return Mail(self.send_sem, self.recv_sem, self.base + base, self.sent)

    def send(self, slot, src, dst, target):
        copy = pltpu.make_async_remote_copy(
            src_ref=src,
            dst_ref=dst,
            send_sem=self.send_sem.at[self.base + slot],
            recv_sem=self.recv_sem.at[self.base + slot],
            device_id=target,
            device_id_type=MESH,
        )
        copy.start()
        self.sent.append(copy)

    def take(self, slot, dst, source):
        pltpu.make_async_remote_copy(
            src_ref=dst,
            dst_ref=dst,
            send_sem=self.send_sem.at[self.base + slot],
            recv_sem=self.recv_sem.at[self.base + slot],
            device_id=source,
            device_id_type=MESH,
        ).wait_recv()

    def finish(self):
        for copy in self.sent:
            copy.wait_send()


class LineGather:
    slots = 9

    def __init__(self, mail, base, spot, plane, full, local_sem):
        self.mail, self.base, self.spot, self.plane, self.full = mail, base, spot, plane, full
        y, c = spot[2:]
        self.own = pltpu.make_async_copy(plane, self.part(y, c), local_sem)

    def part(self, row, core, half=None):
        lead = pl.ds(0, 4) if half is None else pl.ds(2 * half, 2)
        return self.full.at[lead, pl.ds(0, 4), 2 * row + core]

    def send(self, slot, src, dst, target):
        self.mail.send(self.base + slot, src, dst, target)

    def take(self, slot, dst, source):
        self.mail.take(self.base + slot, dst, source)

    def names(self):
        y, c = self.spot[2:]
        return (y, c, up1(y), down1(y), up2(y)) + tuple(ctx_peers(self.spot))

    def step_one(self):
        y, c, yp, ym, y2, to_yp, to_ym, other = self.names()
        self.send(0, self.plane, self.part(y, c), to_yp)
        self.send(1, self.plane, self.part(y, c), to_ym)
        self.send(2, self.plane, self.part(y, c), other)
        self.own.start()

    def step_two(self):
        y, c, yp, ym, y2, to_yp, to_ym, other = self.names()
        self.take(0, self.part(ym, c), to_ym)
        self.send(3, self.part(ym, c, 0), self.part(ym, c, 0), to_yp)
        self.send(4, self.part(ym, c), self.part(ym, c), other)
        self.take(1, self.part(yp, c), to_yp)
        self.send(5, self.part(yp, c, 1), self.part(yp, c, 1), to_ym)
        self.send(6, self.part(yp, c), self.part(yp, c), other)

    def step_three(self):
        y, c, yp, ym, y2, to_yp, to_ym, other = self.names()
        self.take(3, self.part(y2, c, 0), to_ym)
        self.send(7, self.part(y2, c, 0), self.part(y2, c, 0), other)
        self.take(5, self.part(y2, c, 1), to_yp)
        self.send(8, self.part(y2, c, 1), self.part(y2, c, 1), other)

    def step_four(self):
        y, c, yp, ym, y2, to_yp, to_ym, other = self.names()
        self.own.wait()
        self.take(2, self.part(y, 1 - c), other)
        self.take(4, self.part(ym, 1 - c), other)
        self.take(6, self.part(yp, 1 - c), other)
        self.take(7, self.part(y2, 1 - c, 0), other)
        self.take(8, self.part(y2, 1 - c, 1), other)


class PlaneGather:
    slots = 15

    def __init__(self, mail, base, spot, own, full, local_sem):
        self.mail, self.base, self.spot, self.block, self.full = mail, base, spot, own, full
        x, z = spot[:2]
        self.own = pltpu.make_async_copy(own, full.at[:, x, z], local_sem)

    def names(self):
        x, z, y, c = self.spot
        xp, xm, zp, zm = up1(x), down1(x), up1(z), down1(z)
        to = (device(xp, z, y, c), device(xm, z, y, c), device(x, zp, y, c), device(x, zm, y, c))
        return x, z, xp, xm, zp, zm, up2(x), up2(z), to

    def pass_on(self, slot, where, target):
        region = self.full.at[where]
        self.mail.send(self.base + slot, region, region, target)

    def take(self, slot, where, source):
        self.mail.take(self.base + slot, self.full.at[where], source)

    pair, one, two, three = pl.ds(0, 2), pl.ds(0, 1), pl.ds(1, 1), pl.ds(2, 1)
    every, lo, hi = pl.ds(0, 4), pl.ds(0, 2), pl.ds(2, 2)

    def step_one(self):
        x, z, xp, xm, zp, zm, x2, z2, (to_xp, to_xm, to_zp, to_zm) = self.names()
        self.own.start()
        for slot, slabs, target in (
            (0, self.pair, to_xp),
            (1, self.pair, to_xm),
            (2, self.three, to_zp),
            (3, self.three, to_zm),
        ):
            self.mail.send(
                self.base + slot, self.block.at[slabs], self.full.at[slabs, x, z], target
            )

    def step_two(self):
        x, z, xp, xm, zp, zm, x2, z2, (to_xp, to_xm, to_zp, to_zm) = self.names()
        self.take(0, (self.pair, xm, z), to_xm)
        self.pass_on(4, (self.one, xm, z), to_xp)
        self.take(1, (self.pair, xp, z), to_xp)
        self.pass_on(5, (self.two, xp, z), to_xm)
        self.take(2, (self.three, x, zm), to_zm)
        self.pass_on(6, (self.three, x, zm), to_zp)
        self.take(3, (self.three, x, zp), to_zp)

    def step_three(self):
        x, z, xp, xm, zp, zm, x2, z2, (to_xp, to_xm, to_zp, to_zm) = self.names()
        self.take(4, (self.one, x2, z), to_xm)
        self.take(5, (self.two, x2, z), to_xp)
        self.own.wait()
        self.pass_on(7, (self.pair, self.every, z), to_zp)
        self.pass_on(8, (self.pair, self.every, z), to_zm)
        self.take(6, (self.three, x, z2), to_zm)
        self.pass_on(9, (self.three, x, self.every), to_xp)
        self.pass_on(10, (self.three, x, self.every), to_xm)

    def step_four(self):
        x, z, xp, xm, zp, zm, x2, z2, (to_xp, to_xm, to_zp, to_zm) = self.names()
        self.take(7, (self.pair, self.every, zm), to_zm)
        self.pass_on(11, (self.one, self.every, zm), to_zp)
        self.take(8, (self.pair, self.every, zp), to_zp)
        self.pass_on(12, (self.two, self.every, zp), to_zm)
        self.take(9, (self.three, xm, self.every), to_xm)
        self.pass_on(13, (self.three, xm, self.lo), to_xp)
        self.take(10, (self.three, xp, self.every), to_xp)
        self.pass_on(14, (self.three, xp, self.hi), to_xm)

    def step_five(self):
        x, z, xp, xm, zp, zm, x2, z2, (to_xp, to_xm, to_zp, to_zm) = self.names()
        self.take(11, (self.one, self.every, z2), to_zm)
        self.take(12, (self.two, self.every, z2), to_zp)
        self.take(13, (self.three, x2, self.lo), to_xm)
        self.take(14, (self.three, x2, self.hi), to_xp)


def ring_peers(spot):
    x, z, y, c = spot
    return [
        device(up1(x), z, y, c),
        device(down1(x), z, y, c),
        device(x, up1(z), y, c),
        device(x, down1(z), y, c),
    ]


def ctx_peers(spot):
    x, z, y, c = spot
    return [device(x, z, up1(y), c), device(x, z, down1(y), c), device(x, z, y, 1 - c)]


def first_gather_kernel(
    one_ref, qkv_ref, bias_ref, out_ref, two_ref,
    full, plane_out,
    rows, vectors, offsets, plane, send_sem, recv_sem, local_sem,
):
    spot = place()
    x, z, y, c = spot
    index = (x * 4 + z) * 8 + 2 * y + c
    mail = Mail(send_sem, recv_sem)
    vectors[...] = jnp.zeros_like(vectors)
    offsets[...] = jnp.zeros_like(offsets)
    vectors[0:2, 0:7] = one_ref[...].astype(F32)
    vectors[2:4, 0:7] = two_ref[...].astype(F32)
    offsets[0:2, 0:9] = bias_ref[...].astype(F32)
    gains = pltpu.roll(vectors[...], 7 * index, 1)
    bias = pltpu.roll(offsets[...], 9 * index - 128 * lax.div(index, 16), 1)
    for l in range(LAYERS):
        rows[l, 0:7, :] = qkv_ref[l, :, :1024].astype(F32)
        rows[l, 8:15, 0:128] = qkv_ref[l, :, 1024:].astype(F32)
        rows[l, 8:15, 128:1024] = out_ref[l].astype(F32)
        rows[l, 7:8, 0:D] = gains[l : l + 1, :D]
        rows[l, 15:16, 0:D] = gains[2 + l : 3 + l, :D]
        rows[l, 7:8, D:1024] = bias[l : l + 1, :128]
        rows[l, 15:16, D:1024] = bias[l : l + 1, 128:]
    plane[:, x, z] = rows[...].astype(BF)
    xp, xm, zp, zm, x2, z2 = up1(x), down1(x), up1(z), down1(z), up2(x), up2(z)
    to_xp, to_xm, to_zp, to_zm = ring_peers(spot)
    greet(ring_peers(spot) + ctx_peers(spot))

    def pass_on(slot, where, target):
        mail.send(slot, plane.at[where], plane.at[where], target)

    def take(slot, where, source):
        mail.take(slot, plane.at[where], source)

    both, every = pl.ds(0, 2), pl.ds(0, 4)
    pass_on(0, (both, x, z), to_xp)
    pass_on(1, (both, x, z), to_xm)
    take(0, (both, xm, z), to_xm)
    pass_on(2, (0, xm, z), to_xp)
    take(1, (both, xp, z), to_xp)
    pass_on(3, (1, xp, z), to_xm)
    take(2, (0, x2, z), to_xm)
    take(3, (1, x2, z), to_xp)
    pass_on(4, (both, every, z), to_zp)
    pass_on(5, (both, every, z), to_zm)
    take(4, (both, every, zm), to_zm)
    pass_on(6, (0, every, zm), to_zp)
    take(5, (both, every, zp), to_zp)
    pass_on(7, (1, every, zp), to_zm)
    take(6, (0, every, z2), to_zm)
    take(7, (1, every, z2), to_zp)
    line = LineGather(mail, 8, spot, plane.at[0], full, local_sem.at[0])
    line.step_one()
    kept = pltpu.make_async_copy(plane.at[1], plane_out, local_sem.at[1])
    kept.start()
    line.step_two()
    line.step_three()
    line.step_four()
    kept.wait()
    mail.finish()


def first_gather(gain_one, w_qkv, b_qkv, w_out, gain_two):
    return pl.pallas_call(
        first_gather_kernel,
        out_shape=(
            jax.ShapeDtypeStruct((4, 4, 8, 16, 1024), BF),
            jax.ShapeDtypeStruct((4, 4, 16, 1024), BF),
        ),
        in_specs=[pl.BlockSpec(memory_space=pltpu.VMEM)] * 5,
        out_specs=[pl.BlockSpec(memory_space=pl.ANY)] * 2,
        scratch_shapes=[
            pltpu.VMEM((2, 16, 1024), F32),
            pltpu.VMEM((8, 1024), F32),
            pltpu.VMEM((8, 256), F32),
            pltpu.VMEM((2, 4, 4, 16, 1024), BF),
            pltpu.SemaphoreType.DMA((17,)),
            pltpu.SemaphoreType.DMA((17,)),
            pltpu.SemaphoreType.DMA((2,)),
        ],
        compiler_params=pltpu.CompilerParams(
            collective_id=1, has_side_effects=True, vmem_limit_bytes=16 * 1024 * 1024
        ),
        name="first_gather",
    )(gain_one, w_qkv, b_qkv, w_out, gain_two)


class PlaneSum:
    def __init__(self, mail, base, spot, g, cut, buffers):
        self.mail, self.base, self.spot, self.g, self.cut = mail, base, spot, g, cut
        self.count = g.shape[0]
        self.buffers = buffers

    @staticmethod
    def scratch(slabs, cut, rows, columns):
        rest = slabs - cut
        out = [
            pltpu.VMEM((2, cut, 2, rows, columns), BF),
            pltpu.VMEM((2, cut, 4, rows, columns), BF),
            pltpu.VMEM((2, rest, 2, rows, columns), BF),
            pltpu.VMEM((2, rest, 4, rows, columns), BF),
            pltpu.VMEM((2, cut // 2, rows, columns), BF),
            pltpu.VMEM((2, cut, rows, columns), BF),
            pltpu.VMEM((2, max(rest // 2, 1), rows, columns), BF),
            pltpu.VMEM((2, rest, rows, columns), BF),
        ]
        return out

    @staticmethod
    def peers(spot, slabs, cut):
        x, z, y, c = spot
        near = [device(up1(x), z, y, c), device(down1(x), z, y, c), device(x, up1(z), y, c), device(x, down1(z), y, c)]
        return near + ([device(x, up2(z), y, c)] if slabs - cut == 1 else [])

    def names(self):
        x, z, y, c = self.spot
        xp, xm, zp, zm = up1(x), down1(x), up1(z), down1(z)
        to = (device(xp, z, y, c), device(xm, z, y, c), device(x, zp, y, c), device(x, zm, y, c))
        return x, z, xp, xm, zp, zm, up2(x), up2(z), to

    def send(self, slot, src, dst, target):
        self.mail.send(self.base + slot, src, dst, target)

    def take(self, slot, dst, source):
        self.mail.take(self.base + slot, dst, source)

    def add(self, where, extra):
        self.g[where] = (self.g[where].astype(F32) + extra.astype(F32)).astype(BF)

    def step_one(self):
        x, z, xp, xm, zp, zm, x2, z2, (to_xp, to_xm, to_zp, to_zm) = self.names()
        fa, ga, fb, gb, pa, qa, pb, qb = self.buffers
        sa, sb = pl.ds(0, self.cut), pl.ds(self.cut, self.count - self.cut)
        lo, hi = pl.ds(0, 2), pl.ds(2, 2)
        self.send(0, self.g.at[sa, lo, z2], fa.at[0], to_zp)
        self.send(1, self.g.at[sa, hi, z2], fa.at[1], to_zm)
        self.send(2, self.g.at[sb, x2, lo], fb.at[0], to_xp)
        self.send(3, self.g.at[sb, x2, hi], fb.at[1], to_xm)

    def step_two(self):
        x, z, xp, xm, zp, zm, x2, z2, (to_xp, to_xm, to_zp, to_zm) = self.names()
        fa, ga, fb, gb, pa, qa, pb, qb = self.buffers
        sa, sb = pl.ds(0, self.cut), pl.ds(self.cut, self.count - self.cut)
        lo, hi, every = pl.ds(0, 2), pl.ds(2, 2), pl.ds(0, 4)
        self.take(0, fa.at[0], to_zm)
        self.add((sa, lo, zp), fa[0])
        self.send(4, self.g.at[sa, every, zp], ga.at[0], to_zp)
        self.take(2, fb.at[0], to_xm)
        self.add((sb, xp, lo), fb[0])
        self.send(6, self.g.at[sb, xp, every], gb.at[0], to_xp)
        self.take(1, fa.at[1], to_zp)
        self.add((sa, hi, zm), fa[1])
        self.send(5, self.g.at[sa, every, zm], ga.at[1], to_zm)
        self.take(3, fb.at[1], to_xp)
        self.add((sb, xm, hi), fb[1])
        self.send(7, self.g.at[sb, xm, every], gb.at[1], to_xm)

    def step_three(self):
        x, z, xp, xm, zp, zm, x2, z2, (to_xp, to_xm, to_zp, to_zm) = self.names()
        fa, ga, fb, gb, pa, qa, pb, qb = self.buffers
        y, c = self.spot[2:]
        cut, rest = self.cut, self.count - self.cut
        sa, sb = pl.ds(0, cut), pl.ds(cut, rest)
        every = pl.ds(0, 4)
        self.take(4, ga.at[0], to_zm)
        self.take(5, ga.at[1], to_zp)
        self.add((sa, every, z), ga[0].astype(F32) + ga[1].astype(F32))
        self.send(8, self.g.at[pl.ds(0, cut // 2), x2, z], pa.at[0], to_xp)
        self.send(9, self.g.at[pl.ds(cut // 2, cut // 2), x2, z], pa.at[1], to_xm)
        self.take(6, gb.at[0], to_xm)
        self.take(7, gb.at[1], to_xp)
        self.add((sb, x, every), gb[0].astype(F32) + gb[1].astype(F32))
        if rest == 1:
            self.send(10, self.g.at[sb, x, z2], pb.at[0], device(x, z2, y, c))
            self.send(14, self.g.at[sb, x, zp], qb.at[0], to_zp)
            self.send(15, self.g.at[sb, x, zm], qb.at[1], to_zm)
        else:
            self.send(10, self.g.at[pl.ds(cut, rest // 2), x, z2], pb.at[0], to_zp)
            self.send(11, self.g.at[pl.ds(cut + rest // 2, rest // 2), x, z2], pb.at[1], to_zm)

    def step_four(self):
        x, z, xp, xm, zp, zm, x2, z2, (to_xp, to_xm, to_zp, to_zm) = self.names()
        fa, ga, fb, gb, pa, qa, pb, qb = self.buffers
        cut, rest = self.cut, self.count - self.cut
        sa, sb = pl.ds(0, cut), pl.ds(cut, rest)
        self.take(8, pa.at[0], to_xm)
        self.add((pl.ds(0, cut // 2), xp, z), pa[0])
        self.send(12, self.g.at[sa, xp, z], qa.at[0], to_xp)
        self.take(9, pa.at[1], to_xp)
        self.add((pl.ds(cut // 2, cut // 2), xm, z), pa[1])
        self.send(13, self.g.at[sa, xm, z], qa.at[1], to_xm)
        if rest > 1:
            self.take(10, pb.at[0], to_zm)
            self.add((pl.ds(cut, rest // 2), x, zp), pb[0])
            self.send(14, self.g.at[sb, x, zp], qb.at[0], to_zp)
            self.take(11, pb.at[1], to_zp)
            self.add((pl.ds(cut + rest // 2, rest // 2), x, zm), pb[1])
            self.send(15, self.g.at[sb, x, zm], qb.at[1], to_zm)

    def step_five(self, out):
        x, z, xp, xm, zp, zm, x2, z2, (to_xp, to_xm, to_zp, to_zm) = self.names()
        fa, ga, fb, gb, pa, qa, pb, qb = self.buffers
        y, c = self.spot[2:]
        cut, rest = self.cut, self.count - self.cut
        sa, sb = pl.ds(0, cut), pl.ds(cut, rest)
        self.take(12, qa.at[0], to_xm)
        self.take(13, qa.at[1], to_xp)
        out[sa] = (
            self.g[sa, x, z].astype(F32) + qa[0].astype(F32) + qa[1].astype(F32)
        ).astype(out.dtype)
        self.take(14, qb.at[0], to_zm)
        self.take(15, qb.at[1], to_zp)
        total = self.g[sb, x, z].astype(F32) + qb[0].astype(F32) + qb[1].astype(F32)
        if rest == 1:
            self.take(10, pb.at[0], device(x, z2, y, c))
            total = total + pb[0].astype(F32)
        out[sb] = total.astype(out.dtype)


class AttentionSum:
    def __init__(self, mail, base, spot, a_ref, refs, load_sem):
        self.mail, self.base, self.spot, self.a_ref = mail, base, spot, a_ref
        self.mine, self.near, self.block, self.got = refs[:4]
        self.plane = PlaneSum(mail, base + 4, spot, self.mine, 2, refs[4:])
        self.load = pltpu.make_async_copy(a_ref.at[spot[3]], self.mine, load_sem)

    @staticmethod
    def scratch():
        return [
            pltpu.VMEM((4, 4, 4, 16, 1024), BF),
            pltpu.VMEM((4, 4, 4, 16, 1024), BF),
            pltpu.VMEM((4, 16, 1024), BF),
            pltpu.VMEM((3, 16, 1024), BF),
        ] + PlaneSum.scratch(4, 2, 16, 1024)

    slots = 20

    @staticmethod
    def peers(spot):
        x, z, y, c = spot
        return PlaneSum.peers(spot, 4, 2) + [
            device(x, z, up1(y), c),
            device(x, z, up2(y), c),
            device(x, z, down1(y), c),
            device(x, z, y, 1 - c),
        ]

    def start(self):
        x, z, y, c = self.spot
        self.mail.send(self.base, self.a_ref.at[1 - c], self.near, device(x, z, y, 1 - c))

    def cores(self):
        x, z, y, c = self.spot
        self.load.wait()
        self.mail.take(self.base, self.near, device(x, z, y, 1 - c))

        def body(i, carry):
            self.mine[i] = (self.mine[i].astype(F32) + self.near[i].astype(F32)).astype(BF)
            return carry

        lax.fori_loop(0, 4, body, 0)
        self.plane.step_one()

    def rows(self):
        x, z, y, c = self.spot
        self.plane.step_five(self.block)
        for k, step in enumerate((up1, up2, down1)):
            to = device(x, z, step(y), c)
            self.mail.send(self.base + 1 + k, self.block.at[step(y)], self.got.at[k], to)

    def last(self, out):
        x, z, y, c = self.spot
        total = self.block[y].astype(F32)
        for k, step in enumerate((down1, up2, up1)):
            self.mail.take(self.base + 1 + k, self.got.at[k], device(x, z, step(y), c))
            total = total + self.got[k].astype(F32)
        out[...] = total


def nn(left, right):
    return jnp.dot(left, right, preferred_element_type=F32)


def nt(left, right):
    return lax.dot_general(left, right, (((1,), (1,)), ((), ())), preferred_element_type=F32)


def tn(left, right):
    return lax.dot_general(left, right, (((0,), (0,)), ((), ())), preferred_element_type=F32)


def mlp_scratch():
    return [
        pltpu.VMEM((4, 2, 128, D), BF),
        pltpu.VMEM((4, 2, 128, D), BF),
        pltpu.VMEM((4, 128, D), BF),
        pltpu.VMEM((3, 128, D), BF),
        pltpu.VMEM((2, 64, D), BF),
        pltpu.VMEM((2, 64, D), BF),
        pltpu.VMEM((2, 128, D), BF),
    ]


def mlp_exchange(mail, spot, src, buffers, chunk, fillers, hook):
    rows, part, near, own, far, fin, got = buffers
    x, z, y, c = spot
    yp, ym, y2 = up1(y), down1(y), up2(y)
    to_yp, to_ym, other = device(x, z, yp, c), device(x, z, ym, c), device(x, z, y, 1 - c)
    first, second = pl.ds(0, 64), pl.ds(64, 64)
    mail.send(0, src, rows.at[y, c], to_yp)
    mail.send(1, src, rows.at[y, c], to_ym)
    mail.send(2, src, rows.at[y, c], other)
    rows[y, c] = src[...]
    mail.take(2, rows.at[y, 1 - c], other)
    chunk(y)
    mail.send(12, part.at[y, 1 - c], near.at[3], other)
    mail.take(0, rows.at[ym, c], to_ym)
    mail.send(3, rows.at[ym, c, first], rows.at[ym, c, first], to_yp)
    mail.send(4, rows.at[ym, c], rows.at[ym, c], other)
    mail.take(1, rows.at[yp, c], to_yp)
    mail.send(5, rows.at[yp, c, second], rows.at[yp, c, second], to_ym)
    mail.send(6, rows.at[yp, c], rows.at[yp, c], other)
    mail.take(4, rows.at[ym, 1 - c], other)
    chunk(ym)
    mail.send(11, part.at[ym, 1 - c], near.at[2], other)
    hook()
    mail.take(6, rows.at[yp, 1 - c], other)
    chunk(yp)
    mail.send(10, part.at[yp, 1 - c], near.at[1], other)
    mail.take(3, rows.at[y2, c, first], to_ym)
    mail.send(7, rows.at[y2, c, first], rows.at[y2, c, first], other)
    mail.take(5, rows.at[y2, c, second], to_yp)
    mail.send(8, rows.at[y2, c, second], rows.at[y2, c, second], other)
    mail.take(11, near.at[2], other)
    own[2] = (part[ym, c].astype(F32) + near[2].astype(F32)).astype(BF)
    mail.send(16, own.at[2], got.at[1], to_ym)
    mail.take(10, near.at[1], other)
    own[1] = (part[yp, c].astype(F32) + near[1].astype(F32)).astype(BF)
    mail.send(15, own.at[1], got.at[0], to_yp)
    mail.take(7, rows.at[y2, 1 - c, first], other)
    mail.take(8, rows.at[y2, 1 - c, second], other)
    chunk(y2)
    mail.send(9, part.at[y2, 1 - c], near.at[0], other)
    fillers[0]()
    mail.take(9, near.at[0], other)
    own[0] = (part[y2, c].astype(F32) + near[0].astype(F32)).astype(BF)
    mail.send(13, own.at[0, first], far.at[0], to_yp)
    mail.send(14, own.at[0, second], far.at[1], to_ym)
    fillers[1]()
    mail.take(13, far.at[0], to_ym)
    mail.send(17, far.at[0], fin.at[0], to_yp)
    mail.take(14, far.at[1], to_yp)
    mail.send(18, far.at[1], fin.at[1], to_ym)
    fillers[2]()
    mail.take(12, near.at[3], other)
    mail.take(15, got.at[0], to_ym)
    mail.take(16, got.at[1], to_yp)
    mail.take(17, fin.at[0], to_ym)
    mail.take(18, fin.at[1], to_yp)
    total = (
        part[y, c].astype(F32)
        + near[3].astype(F32)
        + got[0].astype(F32)
        + got[1].astype(F32)
    )
    return total + fin[...].reshape(128, D).astype(F32)


def nothing():
    return None


def mlp_backward_kernel(layer, carries, *refs):
    g_ref, w_ref, hr_ref, gate_ref, up_ref = refs[:5]
    refs = refs[5:]
    if carries:
        before, refs = refs[0], refs[1:]
    out_ref, grads = refs[:2]
    refs = refs[2:]
    if carries:
        summed, refs = refs[0], refs[1:]
    buffers, refs = refs[:7], refs[7:]
    w, hr, gate, up, act, src, send_sem, recv_sem, local_sem = refs[:9]
    rows, part = buffers[0], buffers[1]
    spot = place()
    x, z, y, c = spot
    mail = Mail(send_sem, recv_sem)
    loads = [
        pltpu.make_async_copy(a, b, local_sem.at[i])
        for i, (a, b) in enumerate(
            ((w_ref, w), (gate_ref, gate), (up_ref, up), (hr_ref, hr))
        )
    ]
    if carries:
        older = AttentionSum(mail, 19, spot, before, refs[9:], local_sem.at[4])
        loads.append(older.load)
    for load in loads:
        load.start()
    src[...] = g_ref[...].astype(BF)
    greet(AttentionSum.peers(spot) if carries else ctx_peers(spot))
    loaded = []

    def chunk(row):
        if not loaded:
            for load in loads[:3]:
                load.wait()
            loaded.append(True)
        gz = rows[row].reshape(256, D)
        gact = nn(gz, w[2])
        g = gate[row].astype(F32)
        u = up[row].astype(F32)
        s = 1.0 / (1.0 + jnp.exp(-g))
        silu = g * s
        act[row] = (silu * u).astype(BF)
        gg = (gact * u * (s + silu * (1.0 - s))).astype(BF)
        gu = (gact * silu).astype(BF)
        gate[row] = gg
        up[row] = gu
        part[row] = (nt(gg, w[0]) + nt(gu, w[1])).astype(BF).reshape(2, 128, D)

    def weight_grad(member, left, right):
        def run():
            r = right[...].reshape(1024, FS)
            for i in range(7):
                l = left[:, :, :, 128 * i : 128 * (i + 1)].reshape(1024, 128)
                grads[member, 128 * i : 128 * (i + 1)] = tn(l, r).astype(BF)

        return run

    def gates():
        loads[3].wait()
        weight_grad(0, hr, gate)()

    fillers = [weight_grad(2, rows, act), gates, weight_grad(1, hr, up)]
    hook = nothing
    if carries:
        older.start()
        hook = older.cores
        steps = [older.plane.step_two, older.plane.step_three, older.plane.step_four]

        def joined(step, filler):
            def run():
                step()
                filler()

            return run

        fillers = [joined(step, filler) for step, filler in zip(steps, fillers)]
    out_ref[...] = mlp_exchange(mail, spot, src, buffers, chunk, fillers, hook)
    if carries:
        older.rows()
        older.last(summed)
    mail.finish()


def mlp_backward(layer, grad_output, m_full, hidden_rows, gate, up, before):
    anywhere = pl.BlockSpec(memory_space=pl.ANY)
    vmem = pl.BlockSpec(memory_space=pltpu.VMEM)
    carries = before is not None
    out_shape = [jax.ShapeDtypeStruct((128, D), F32), jax.ShapeDtypeStruct((3, D, FS), BF)]
    scratch = mlp_scratch() + [
        pltpu.VMEM((3, D, FS), BF),
        pltpu.VMEM((4, 2, 128, D), BF),
        pltpu.VMEM((4, 256, FS), BF),
        pltpu.VMEM((4, 256, FS), BF),
        pltpu.VMEM((4, 256, FS), BF),
        pltpu.VMEM((128, D), BF),
        pltpu.SemaphoreType.DMA((39,)),
        pltpu.SemaphoreType.DMA((39,)),
        pltpu.SemaphoreType.DMA((5,)),
    ]
    operands = [grad_output, m_full, hidden_rows, gate, up]
    if carries:
        out_shape.append(jax.ShapeDtypeStruct((16, 1024), F32))
        scratch += AttentionSum.scratch()
        operands.append(before)
    return pl.pallas_call(
        functools.partial(mlp_backward_kernel, layer, carries),
        out_shape=tuple(out_shape),
        in_specs=[vmem] + [anywhere] * (len(operands) - 1),
        out_specs=[vmem] * len(out_shape),
        scratch_shapes=scratch,
        compiler_params=pltpu.CompilerParams(
            collective_id=10 + layer, has_side_effects=True, vmem_limit_bytes=52 * 1024 * 1024
        ),
        name="mlp_backward_%d" % layer,
    )(*operands)


def last_sum_kernel(a_ref, out_ref, *refs):
    send_sem, recv_sem, local_sem = refs[-3:]
    spot = place()
    mail = Mail(send_sem, recv_sem)
    older = AttentionSum(mail, 0, spot, a_ref, refs[:-3], local_sem.at[0])
    older.load.start()
    greet(AttentionSum.peers(spot))
    older.start()
    older.cores()
    older.plane.step_two()
    older.plane.step_three()
    older.plane.step_four()
    older.rows()
    older.last(out_ref)
    mail.finish()


def last_sum(a_grads):
    return pl.pallas_call(
        last_sum_kernel,
        out_shape=jax.ShapeDtypeStruct((16, 1024), F32),
        in_specs=[pl.BlockSpec(memory_space=pl.ANY)],
        out_specs=pl.BlockSpec(memory_space=pltpu.VMEM),
        scratch_shapes=AttentionSum.scratch()
        + [
            pltpu.SemaphoreType.DMA((20,)),
            pltpu.SemaphoreType.DMA((20,)),
            pltpu.SemaphoreType.DMA((1,)),
        ],
        compiler_params=pltpu.CompilerParams(
            collective_id=2, has_side_effects=True, vmem_limit_bytes=32 * 1024 * 1024
        ),
        name="last_sum",
    )(a_grads)


def swap_halves(u):
    width = u.shape[1]
    lane = lax.broadcasted_iota(jnp.int32, u.shape, 1)
    return jnp.where(
        lax.rem(lane, 64) < 32, pltpu.roll(u, width - 32, 1), pltpu.roll(u, 32, 1)
    )


def normal(v):
    r = lax.rsqrt(jnp.mean(v * v, axis=-1, keepdims=True) + eps_norm)
    return v * r, r


def forward_kernel(layer, *refs):
    x_ref, a_ref, m_ref, pick_ref, cos_ref, sin_ref, qpos_ref, kpos_ref = refs[:8]
    refs = refs[8:]
    if layer == 0:
        plane_ref, refs = refs[0], refs[1:]
    out_ref, vec_ref, mid_ref, att_ref, qs_ref, kvs_ref, probs_ref, low_ref, high_ref = refs[:9]
    hr_ref, gate_ref, up_ref = refs[9:12]
    refs = refs[12:]
    if layer == 0:
        m_zero, m_one, a_one = refs[:3]
        refs = refs[3:]
    blocks, low, high, kv, kvs, probs, heads, mask, att, qs, mid, h2 = refs[:12]
    buffers, refs = refs[12:19], refs[19:]
    w, gate, up, send_sem, recv_sem, local_sem = refs[:6]
    rows, part = buffers[0], buffers[1]
    spot = place()
    x, z, y, c = spot
    mail = Mail(send_sem, recv_sem)
    load = pltpu.make_async_copy(a_ref, blocks, local_sem.at[0])
    load.start()
    if layer == 0:
        line = LineGather(mail, 28, spot, plane_ref, a_one, local_sem.at[21])
        now = PlaneGather(mail, 37, spot, m_ref.at[0], m_zero, local_sem.at[22])
        later = PlaneGather(mail, 52, spot, m_ref.at[1], m_one, local_sem.at[23])
        greet(ctx_peers(spot) + ring_peers(spot))
        now.step_one()
        line.step_one()
    else:
        load_w = pltpu.make_async_copy(m_ref, w, local_sem.at[1])
        load_w.start()
        greet(ctx_peers(spot))
    inputs = x_ref[...]
    n, r = normal(inputs)
    load.wait()
    spare = []
    for g in range(8):
        group = blocks[g // 2, 2 * (g % 2) : 2 * (g % 2) + 2].reshape(256, 1024)
        low[112 * g : 112 * (g + 1)] = nn(pick_ref[0:112, :], group).astype(BF)
        high[112 * g : 112 * (g + 1)] = nn(pick_ref[112:224, :], group).astype(BF)
        spare.append(nn(pick_ref[224:240, :], group))
    gains = functools.reduce(lambda u, v: u + v, [block[0:2, :D] for block in spare])
    vec_ref[0:2, 0:D] = gains
    for j in range(9):
        piece = jnp.zeros((1, 128), F32)
        if j < 8:
            piece = piece + spare[j][0:1, D:]
        if j > 0:
            piece = piece + spare[j - 1][1:2, D:]
        vec_ref[2:3, 128 * j : 128 * (j + 1)] = piece
    stores = [
        pltpu.make_async_copy(low, low_ref, local_sem.at[2]),
        pltpu.make_async_copy(high, high_ref, local_sem.at[3]),
    ]
    hidden = (n * gains[0:1]).astype(BF)
    packed = nn(hidden, low[...]) + vec_ref[2:3, :1024]
    values = nn(hidden, high[:, :128]) + vec_ref[2:3, 1024:]
    turned = packed * cos_ref[...] + swap_halves(packed) * sin_ref[...]
    kv[y, c, :, 0:128] = turned[:, D:].astype(BF)
    kv[y, c, :, 128:256] = values.astype(BF)
    yp, ym, y2 = up1(y), down1(y), up2(y)
    to_yp, to_ym, other = ctx_peers(spot)
    first, second = pl.ds(0, 64), pl.ds(64, 64)
    mail.send(0, kv.at[y, c], kv.at[y, c], to_yp)
    mail.send(1, kv.at[y, c], kv.at[y, c], to_ym)
    mail.send(2, kv.at[y, c], kv.at[y, c], other)
    for store in stores:
        store.start()
    if layer == 0:
        now.step_two()
    for h in range(H):
        qs[h] = (turned[:, HD * h : HD * (h + 1)] * HD ** (-0.5)).astype(BF)
    mask[...] = jnp.where(kpos_ref[...] <= qpos_ref[...], 0.0, 1.0)
    mail.take(0, kv.at[ym, c], to_ym)
    mail.send(3, kv.at[ym, c, first], kv.at[ym, c, first], to_yp)
    mail.send(4, kv.at[ym, c], kv.at[ym, c], other)
    mail.take(1, kv.at[yp, c], to_yp)
    mail.send(5, kv.at[yp, c, second], kv.at[yp, c, second], to_ym)
    mail.send(6, kv.at[yp, c], kv.at[yp, c], other)
    mail.take(3, kv.at[y2, c, first], to_ym)
    mail.send(7, kv.at[y2, c, first], kv.at[y2, c, first], other)
    mail.take(5, kv.at[y2, c, second], to_yp)
    mail.send(8, kv.at[y2, c, second], kv.at[y2, c, second], other)
    if layer == 0:
        now.step_three()
    mail.take(2, kv.at[y, 1 - c], other)
    mail.take(4, kv.at[ym, 1 - c], other)
    mail.take(6, kv.at[yp, 1 - c], other)
    mail.take(7, kv.at[y2, 1 - c, first], other)
    mail.take(8, kv.at[y2, 1 - c, second], other)
    for i in range(4):
        kvs[i] = kv[:, :, :, HD * i : HD * (i + 1)].reshape(1024, HD)

    def body(i, carry):
        for k in range(KVH):
            h = i + 7 * k
            scores = nt(qs[h], kvs[k])
            scores = jnp.where(mask[...] > 0.5, neg_fill, scores)
            e = jnp.exp(scores - jnp.max(scores, axis=-1, keepdims=True))
            p = (e * (1.0 / jnp.sum(e, axis=-1, keepdims=True))).astype(BF)
            probs[h] = p
            heads[h] = nn(p, kvs[2 + k]).astype(BF)
        return carry

    lax.fori_loop(0, 4, body, 0)
    if layer == 0:
        line.step_two()
    lax.fori_loop(4, 7, body, 0)
    if layer == 0:
        now.step_four()
    att[...] = jnp.concatenate([heads[h] for h in range(H)], axis=1)
    mid[...] = inputs + nn(att[...], high[:, 128:])
    h2[...] = (normal(mid[...])[0] * gains[1:2]).astype(BF)
    for i, (src, dst) in enumerate(
        ((kvs, kvs_ref), (probs, probs_ref), (att, att_ref), (qs, qs_ref), (mid, mid_ref))
    ):
        stores.append(pltpu.make_async_copy(src, dst, local_sem.at[4 + i]))
        stores[-1].start()
    if layer == 0:
        line.step_three()
        now.step_five()
        slabs = refs[6]
        load_w = pltpu.make_async_copy(m_zero, slabs, local_sem.at[1])
        load_w.start()
        later.step_one()

    loaded = []

    def chunk(row):
        if not loaded:
            load_w.wait()
            if layer == 0:
                for member in range(3):
                    for i in range(16):
                        w[member, 56 * i : 56 * (i + 1)] = slabs[member, i // 4, i % 4]
            loaded.append(True)
        h = rows[row].reshape(256, D)
        g = nn(h, w[0])
        u = nn(h, w[1])
        gate[row] = g.astype(BF)
        up[row] = u.astype(BF)
        act = (g / (1.0 + jnp.exp(-g)) * u).astype(BF)
        part[row] = nt(act, w[2]).astype(BF).reshape(2, 128, D)
        k = 9 + 3 * (len(loaded) - 1)
        loaded.append(True)
        for i, (src, dst) in enumerate(((rows, hr_ref), (gate, gate_ref), (up, up_ref))):
            stores.append(pltpu.make_async_copy(src.at[row], dst.at[row], local_sem.at[k + i]))
            stores[-1].start()

    steps = [nothing] * 4
    if layer == 0:
        steps = [later.step_two, later.step_three, later.step_four, nothing]
    total = mlp_exchange(mail.shifted(9), spot, h2, buffers, chunk, steps[1:], steps[0])
    out_ref[...] = mid[...] + total
    if layer == 0:
        later.step_five()
        line.step_four()
    for store in stores:
        store.wait()
    mail.finish()


def forward(layer, state, a_full, m_full, pick, tables, positions, plane):
    anywhere = pl.BlockSpec(memory_space=pl.ANY)
    vmem = pl.BlockSpec(memory_space=pltpu.VMEM)
    out_shape = [
        jax.ShapeDtypeStruct((128, D), F32),
        jax.ShapeDtypeStruct((8, QKV), F32),
        jax.ShapeDtypeStruct((128, D), F32),
        jax.ShapeDtypeStruct((128, D), BF),
        jax.ShapeDtypeStruct((H, 128, HD), BF),
        jax.ShapeDtypeStruct((4, 1024, HD), BF),
        jax.ShapeDtypeStruct((H, 128, 1024), BF),
        jax.ShapeDtypeStruct((D, 1024), BF),
        jax.ShapeDtypeStruct((D, 1024), BF),
        jax.ShapeDtypeStruct((4, 2, 128, D), BF),
        jax.ShapeDtypeStruct((4, 256, FS), BF),
        jax.ShapeDtypeStruct((4, 256, FS), BF),
    ]
    operands = [state, a_full, m_full, pick, *tables, *positions]
    in_specs = [vmem, anywhere, anywhere] + [vmem] * 5
    slots = 28
    if layer == 0:
        out_shape += [
            jax.ShapeDtypeStruct((3, 4, 4, 56, FS), BF),
            jax.ShapeDtypeStruct((3, 4, 4, 56, FS), BF),
            jax.ShapeDtypeStruct((4, 4, 8, 16, 1024), BF),
        ]
        operands.append(plane)
        in_specs.append(anywhere)
        slots = 67
    slabs = [pltpu.VMEM((3, 4, 4, 56, FS), BF)] if layer == 0 else []
    return pl.pallas_call(
        functools.partial(forward_kernel, layer),
        out_shape=tuple(out_shape),
        in_specs=in_specs,
        out_specs=[vmem] * 2 + [anywhere] * (len(out_shape) - 2),
        scratch_shapes=[
            pltpu.VMEM((4, 4, 8, 16, 1024), BF),
            pltpu.VMEM((D, 1024), BF),
            pltpu.VMEM((D, 1024), BF),
            pltpu.VMEM((4, 2, 128, 256), BF),
            pltpu.VMEM((4, 1024, HD), BF),
            pltpu.VMEM((H, 128, 1024), BF),
            pltpu.VMEM((H, 128, HD), BF),
            pltpu.VMEM((128, 1024), F32),
            pltpu.VMEM((128, D), BF),
            pltpu.VMEM((H, 128, HD), BF),
            pltpu.VMEM((128, D), F32),
            pltpu.VMEM((128, D), BF),
        ]
        + mlp_scratch()
        + [
            pltpu.VMEM((3, D, FS), BF),
            pltpu.VMEM((4, 256, FS), BF),
            pltpu.VMEM((4, 256, FS), BF),
            pltpu.SemaphoreType.DMA((slots,)),
            pltpu.SemaphoreType.DMA((slots,)),
            pltpu.SemaphoreType.DMA((24,)),
        ]
        + slabs,
        compiler_params=pltpu.CompilerParams(
            collective_id=12 + layer, has_side_effects=True, vmem_limit_bytes=56 * 1024 * 1024
        ),
        name="forward_layer_%d" % layer,
    )(*operands)


def attention_backward_kernel(
    g_ref, ghid2_ref, mid_ref, x_ref, vec_ref, cos_ref, sin_ref, place_ref, att_ref, qs_ref,
    kvs_ref, probs_ref, low_ref, high_ref, m_ref,
    gin_ref, a_out, m_out,
    low, high, kvs, probs, m, gs, gatt, gqs, part, near, own, got, glow, ghigh, special,
    *refs,
):
    send_sem, recv_sem, local_sem = refs[-3:]
    spot = place()
    x, z, y, c = spot
    mail = Mail(send_sem, recv_sem)
    loads = [
        pltpu.make_async_copy(src, dst, local_sem.at[i])
        for i, (src, dst) in enumerate(
            ((m_ref, m), (high_ref, high), (probs_ref, probs), (kvs_ref, kvs), (low_ref, low))
        )
    ]
    for load in loads:
        load.start()
    plane = PlaneSum(mail, 7, spot, m, 2, refs[:-3])
    yp, ym, y2 = up1(y), down1(y), up2(y)
    to_yp, to_ym, other = ctx_peers(spot)
    to_y2 = device(x, z, y2, c)
    greet([to_yp, to_ym, other, to_y2] + PlaneSum.peers(spot, 3, 2))
    loads[0].wait()
    plane.step_one()
    mid = mid_ref[...]
    n, r = normal(mid)
    ghid2 = ghid2_ref[...]
    t = ghid2 * vec_ref[1:2, :D]
    gmid = g_ref[...] + r * (t - n * jnp.mean(t * n, axis=-1, keepdims=True))
    ggain_two = jnp.sum(ghid2 * n, axis=0, keepdims=True)
    gy = gmid.astype(BF)
    loads[1].wait()
    ga = nt(gy, high[:, 128:]).astype(BF)
    for h in range(H):
        gatt[h] = ga[:, HD * h : HD * (h + 1)]
    ghigh[:, 128:] = tn(att_ref[...], gy).astype(BF)
    loads[2].wait()
    loads[3].wait()

    def body(i, carry):
        for k in range(KVH):
            h = i + 7 * k
            p = probs[h].astype(F32)
            gp = nt(gatt[h], kvs[2 + k])
            s = (p * (gp - jnp.sum(gp * p, axis=-1, keepdims=True))).astype(BF)
            gs[h] = s
            gqs[h] = nn(s, kvs[k])
        return carry

    lax.fori_loop(0, 7, body, 0)
    plane.step_two()
    for k in range(KVH):
        heads = pl.ds(7 * k, 7)
        gk = tn(qs_ref[heads].reshape(D, HD), gs[heads].reshape(D, 1024)).astype(BF)
        gv = tn(gatt[heads].reshape(D, HD), probs[heads].reshape(D, 1024)).astype(BF)
        for j in range(8):
            part[j // 2, j % 2, HD * k : HD * (k + 1)] = gk[:, 128 * j : 128 * (j + 1)]
            part[j // 2, j % 2, 128 + HD * k : 128 + HD * (k + 1)] = gv[:, 128 * j : 128 * (j + 1)]
    mail.send(0, part.at[:, 1 - c], near, other)
    gq = jnp.concatenate([gqs[h] for h in range(H)], axis=1) * HD ** (-0.5)
    gq = (gq * cos_ref[:, :D] - swap_halves(gq) * sin_ref[:, :D]).astype(BF)
    inputs = x_ref[...]
    n, r = normal(inputs)
    hidden = (n * vec_ref[0:1, :D]).astype(BF)
    mail.take(0, near, other)
    own[...] = (part[:, c].astype(F32) + near[...].astype(F32)).astype(BF)
    mail.send(1, own.at[yp], got.at[0], to_yp)
    mail.send(2, own.at[ym], got.at[1], to_ym)
    mail.send(3, own.at[y2], got.at[2], to_y2)
    glow[:, :D] = tn(hidden, gq).astype(BF)
    loads[4].wait()
    ghid = nt(gq, low[:, :D])
    plane.step_three()
    mail.take(1, got.at[0], to_ym)
    mail.take(2, got.at[1], to_yp)
    mail.take(3, got.at[2], to_y2)
    total = own[y].astype(F32) + got[0].astype(F32) + got[1].astype(F32) + got[2].astype(F32)
    total = total.T
    gk = total[:, :128]
    gk = (gk * cos_ref[:, D:] - swap_halves(gk) * sin_ref[:, D:]).astype(BF)
    gv = total[:, 128:].astype(BF)
    ghid = ghid + nt(gk, low[:, D:]) + nt(gv, high[:, :128])
    glow[:, D:] = tn(hidden, gk).astype(BF)
    ghigh[:, :128] = tn(hidden, gv).astype(BF)
    t = ghid * vec_ref[0:1, :D]
    gin_ref[...] = gmid + r * (t - n * jnp.mean(t * n, axis=-1, keepdims=True))
    ggain_one = jnp.sum(ghid * n, axis=0, keepdims=True)
    plane.step_four()
    bias_q = jnp.sum(gq.astype(F32), axis=0, keepdims=True)
    bias_k = jnp.sum(gk.astype(F32), axis=0, keepdims=True)
    bias_v = jnp.sum(gv.astype(F32), axis=0, keepdims=True)
    bias = jnp.concatenate([bias_q, bias_k], axis=1)
    row = lax.broadcasted_iota(jnp.int32, (16, 1024), 0)
    row_last = jnp.concatenate([ggain_two, bias_v], axis=1)
    for g in range(8):
        row_seven = jnp.concatenate([ggain_one, bias[:, 128 * g : 128 * (g + 1)]], axis=1)
        extra = jnp.where(row == 0, row_seven, jnp.where(row == 1, row_last, 0.0))
        special[...] = extra.astype(BF)
        block = (
            nn(place_ref[0], glow[112 * g : 112 * (g + 1)])
            + nn(place_ref[1], ghigh[112 * g : 112 * (g + 1)])
            + nn(place_ref[2, :, 0:16], special[...])
        ).astype(BF)
        for k in range(16):
            ctx = k % 8
            a_out[ctx % 2, ctx // 2, g // 2, 2 * (g % 2) + k // 8] = block[16 * k : 16 * (k + 1)]
    plane.step_five(m_out)
    mail.finish()


def attention_backward(layer, grad_output, grad_hidden_two, kept, vectors, tables, place_rows, m_grads):
    x, mid, att, qs, kvs, probs, low, high = kept
    anywhere = pl.BlockSpec(memory_space=pl.ANY)
    vmem = pl.BlockSpec(memory_space=pltpu.VMEM)
    return pl.pallas_call(
        attention_backward_kernel,
        out_shape=(
            jax.ShapeDtypeStruct((128, D), F32),
            jax.ShapeDtypeStruct((2, 4, 4, 4, 16, 1024), BF),
            jax.ShapeDtypeStruct((3, 56, FS), F32),
        ),
        in_specs=[vmem] * 10 + [anywhere] * 5,
        out_specs=[vmem] * 3,
        scratch_shapes=[
            pltpu.VMEM((D, 1024), BF),
            pltpu.VMEM((D, 1024), BF),
            pltpu.VMEM((4, 1024, HD), BF),
            pltpu.VMEM((H, 128, 1024), BF),
            pltpu.VMEM((3, 4, 4, 56, FS), BF),
            pltpu.VMEM((H, 128, 1024), BF),
            pltpu.VMEM((H, 128, HD), BF),
            pltpu.VMEM((H, 128, HD), F32),
            pltpu.VMEM((4, 2, 256, 128), BF),
            pltpu.VMEM((4, 256, 128), BF),
            pltpu.VMEM((4, 256, 128), BF),
            pltpu.VMEM((3, 256, 128), BF),
            pltpu.VMEM((D, 1024), BF),
            pltpu.VMEM((D, 1024), BF),
            pltpu.VMEM((16, 1024), BF),
        ]
        + PlaneSum.scratch(3, 2, 56, FS)
        + [
            pltpu.SemaphoreType.DMA((23,)),
            pltpu.SemaphoreType.DMA((23,)),
            pltpu.SemaphoreType.DMA((5,)),
        ],
        compiler_params=pltpu.CompilerParams(
            collective_id=14 + layer, has_side_effects=True, vmem_limit_bytes=56 * 1024 * 1024
        ),
        name="attention_backward_%d" % layer,
    )(
        grad_output, grad_hidden_two, mid, x, vectors, *tables, place_rows, att, qs,
        kvs, probs, low, high, m_grads.reshape(3, 4, 4, 56, FS),
    )


def select_matrix():
    pick = np.zeros((226, 256), np.float32)
    for k in range(16):
        for r in range(7):
            pick[7 * k + r, 16 * k + r] = 1
            pick[112 + 7 * k + r, 16 * k + 8 + r] = 1
        pick[224, 16 * k + 7] = 1
        pick[225, 16 * k + 15] = 1
    return pick


def assemble_kernel(a_zero, a_one, m_zero, m_one, g_one, g_qkv, g_qk, g_value, g_out, g_two, g_gate, g_up, rows):
    index = lax.axis_index("dp") * 8 + lax.axis_index("ctx")
    rows[...] = jnp.zeros_like(rows)
    for l, (a_ref, m_ref) in enumerate(((a_zero, m_zero), (a_one, m_one))):
        g_qkv[l, :, 0:1024] = a_ref[0:7, :]
        g_qkv[l, :, 1024:1152] = a_ref[8:15, 0:128]
        g_out[l] = a_ref[8:15, 128:1024]
        g_gate[l] = m_ref[0]
        g_up[l] = m_ref[1]
        rows[l : l + 1] = a_ref[7:8, :]
        rows[2 + l : 3 + l] = a_ref[15:16, :]
    gains = pltpu.roll(rows[...], lax.rem(1024 - 7 * index, 1024), 1)
    g_one[...] = gains[0:2, 0:7]
    g_two[...] = gains[2:4, 0:7]
    g_qk[...] = pltpu.roll(rows[...], 128 - 8 * lax.rem(index, 16), 1)[0:2, 0:8]
    g_value[...] = pltpu.roll(rows[...], 128 - index, 1)[2:4, 0:1]


def assemble(a_sums, m_sums):
    vmem = pl.BlockSpec(memory_space=pltpu.VMEM)
    shapes = ((2, 7), (2, 7, QKV), (2, 8), (2, 1), (2, 7, D), (2, 7), (2, 56, FS), (2, 56, FS))
    return pl.pallas_call(
        assemble_kernel,
        out_shape=tuple(jax.ShapeDtypeStruct(shape, F32) for shape in shapes),
        in_specs=[vmem] * 4,
        out_specs=[vmem] * len(shapes),
        scratch_shapes=[pltpu.VMEM((8, 1024), F32)],
        name="assemble",
    )(*a_sums, *m_sums)


def shards(
    tokens, cotangent, span_order, gain_one, w_qkv, b_qkv, w_out, gain_two, w_gate, w_up, w_down
):
    sequences, local_len, width = tokens.shape
    span_len = local_len // 2
    ctx_place = lax.axis_index("ctx")
    offsets = jnp.arange(span_len, dtype=jnp.int32)
    local_spans = lax.dynamic_slice_in_dim(span_order, 2 * ctx_place, 2)
    local_pos = (local_spans[:, None] * span_len + offsets[None, :]).reshape(local_len)
    all_pos = (span_order[:, None] * span_len + offsets[None, :]).reshape(-1)
    positions = (local_pos[:, None], all_pos[None, :])
    frequency = rope_base ** (-jnp.arange(HD // 2, dtype=F32) * 2.0 / HD)
    angles = local_pos.astype(F32)[:, None] * frequency[None, :]
    cosine, sine = jnp.cos(angles), jnp.sin(angles)
    tables = (jnp.tile(cosine, (1, 32)), jnp.tile(jnp.concatenate([-sine, sine], axis=1), (1, 16)))
    chosen = select_matrix()
    pick = jnp.asarray(np.concatenate([chosen, np.zeros((14, 256), np.float32)]), BF)
    spread = np.zeros((3, 256, 112), np.float32)
    spread[0], spread[1], spread[2, :, :2] = chosen[:112].T, chosen[112:224].T, chosen[224:].T
    spread = jnp.asarray(spread, BF)

    m_block = jnp.stack([w_gate, w_up, w_down.transpose(0, 2, 1)], axis=1)
    a_zero, plane_one = first_gather(gain_one, w_qkv, b_qkv, w_out, gain_two)
    state_zero = tokens.reshape(local_len, width).astype(F32)
    state_one, *saved_zero, m_zero, m_one, a_one = forward(
        0, state_zero, a_zero, m_block, pick, tables, positions, plane_one
    )
    m_full = (m_zero.reshape(3, D, FS), m_one.reshape(3, D, FS))
    state, *saved_one = forward(1, state_one, a_one, m_full[1], pick, tables, positions, None)
    vectors = (saved_zero[0], saved_one[0])
    kept_layers = [
        ((state_zero,) + tuple(saved_zero[1:8]), saved_zero[8:]),
        ((state_one,) + tuple(saved_one[1:8]), saved_one[8:]),
    ]
    grad_state = cotangent.reshape(local_len, width).astype(F32)
    a_grads = None
    sums = [None, None]
    a_sums = [None, None]
    for l in reversed(range(LAYERS)):
        kept, kept_mlp = kept_layers[l]
        grad_hidden_two, m_grads, *older = mlp_backward(l, grad_state, m_full[l], *kept_mlp, a_grads)
        if older:
            a_sums[l + 1] = older[0]
        grad_state, a_grads, sums[l] = attention_backward(
            l, grad_state, grad_hidden_two, kept, vectors[l], tables, spread, m_grads
        )
    a_sums[0] = last_sum(a_grads)
    stacks = tuple(assemble(a_sums, sums)) + (jnp.stack([sums[0][2].T, sums[1][2].T]),)
    output = state.astype(BF).reshape(sequences, local_len, width)
    input_grad = grad_state.reshape(sequences, local_len, width)
    return (output, input_grad) + stacks


def solution(mesh):
    return jax.shard_map(
        shards,
        mesh=mesh,
        in_specs=(
            P("dp", "ctx", None),
            P("dp", "ctx", None),
            P(),
            P(None, ("dp", "ctx")),
            P(None, ("dp", "ctx"), None),
            P(None, ("dp", "ctx")),
            P(None, ("dp", "ctx"), None),
            P(None, ("dp", "ctx")),
            P(None, "dp", "ctx"),
            P(None, "dp", "ctx"),
            P(None, "ctx", "dp"),
        ),
        out_specs=(
            P("dp", "ctx", None),
            P("dp", "ctx", None),
            P(None, ("dp", "ctx")),
            P(None, ("dp", "ctx"), None),
            P(None, ("dp", "ctx")),
            P(None, ("dp", "ctx")),
            P(None, ("dp", "ctx"), None),
            P(None, ("dp", "ctx")),
            P(None, "dp", "ctx"),
            P(None, "dp", "ctx"),
            P(None, "ctx", "dp"),
        ),
        check_vma=False,
    )
```

profile of v0, /device:TPU:0, one launch (start us, length us, event | category | flops | bytes accessed | tf_op | source)
XLA Modules:
  0.0 386.1 jit_solution(9078566038829264473)
XLA Ops:
  0.6 0.0 copy-start.14
  0.7 1.7 bitcast_convert_fusion.refs_0_.x_ref
  2.4 0.8 copy.31.qkv_ref
  3.2 0.7 copy.32.out_ref
  3.9 0.0 copy-start.9
  3.9 0.7 copy-done.9
  4.6 0.0 copy-start.10
  4.6 0.7 copy-done.10
  5.2 0.0 copy-start.11
  5.2 0.7 copy-done.11
  5.9 44.0 %first_gather.1 = (bf16[4,4,8,16,1024]{4,3,2,1,0:T(8,128)(2,1)S(1)}, bf16[4,4,16,1024]{3,2,1,0:T(8,128)(2,1)S(1)}) custom-call(bf16[2,7]{1,0:T(2,128)(2,1)S(1)} %copy-done.9, bf16[2,7,1152]{2,1,0:T(8,128)(2,1)S(1)} %copy.31.qkv_ref, bf16[2,9]{1,0:T(2,128)(2,1)S(1)} %copy-done.10, bf16[2,7,896]{2,1,0:T(8,128)(2,1)S(1)} %copy.32.out_ref, ...), custom_call_target="tpu_custom_call" | custom-call | tf_op jit(solution)/shard_map/first_gather/pallas_call | solution.py:304
  49.8 0.0 copy-start
  49.8 2.0 copy-done
  51.9 0.0 copy-start.4
  51.9 0.8 copy-done.4
  52.7 1.9 pad_maximum_fusion.refs_2_
  54.6 0.7 dynamic-slice_multiply_fusion
  55.3 0.1 iota_add_fusion.1
  55.4 0.1 convert_element_type.26
  55.4 0.1 fusion
  55.6 0.1 tile.8
  55.7 1.0 copy.33.refs_4_.cos_ref
  56.7 1.0 copy.34.refs_5_.sin_ref
  57.7 0.8 add.63.refs_6_
  58.5 0.0 copy-done.14
  58.5 0.1 iota_add_fusion
  58.6 0.7 add.62.refs_7_
  59.2 81.4 %forward_layer_0.1 = (f32[128,896]{1,0:T(8,128)}, f32[8,1152]{1,0:T(8,128)}, f32[128,896]{1,0:T(8,128)}, bf16[128,896]{1,0:T(8,128)(2,1)}, bf16[14,128,64]{2,1,0...) custom-call(f32[128,896]{1,0:T(8,128)} %bitcast_convert_fusion.refs_, ...), custom_call_target="tpu_custom_call" | custom-call | tf_op jit(solution)/shard_map/forward_layer_0/pallas_call | solution.py:970
  140.6 0.0 copy-start.13
  140.6 51.1 %forward_layer_1.1 = (f32[128,896]{1,0:T(8,128)}, f32[8,1152]{1,0:T(8,128)}, f32[128,896]{1,0:T(8,128)}, bf16[128,896]{1,0:T(8,128)(2,1)}, bf16[14,128,64]{2,1,0...) custom-call(f32[128,896]{1,0:T(8,128)} %get-tuple-element.61.refs_0_, ...), custom_call_target="tpu_custom_call" | custom-call | tf_op jit(solution)/shard_map/forward_layer_1/pallas_call | solution.py:970
  191.8 1.7 convert_bitcast_fusion
  193.5 0.0 copy-done.13
  193.6 0.0 copy-start.2
  193.6 28.9 %mlp_backward_1.1 = (f32[128,896]{1,0:T(8,128)S(1)}, bf16[3,896,608]{2,1,0:T(8,128)(2,1)}) custom-call(f32[128,896]{1,0:T(8,128)S(1)} %bitcast_convert_fusion.1.refs_0_.g_ref, bf16[3,896,608]{2,1,0:T(8,128)(2,1)} %bitcast.33, bf16[4,2,128,896]{3,2,1,0:T(8,128)(2,1)} %get-tuple-element.65.refs_2_, bf16[4,256,608]{2,1,0:T(8,128)(2,1)} %get-tuple-element.66.refs_3_, ...), custom_call_target="tpu_custom_call" | custom-call | tf_op jit(solution)/shard_map/mlp_backward_1/pallas_call | solution.py:717
  222.5 0.0 copy-done.2
  222.5 0.0 copy-start.6
  222.5 0.8 copy-done.6
  223.3 39.0 %attention_backward_1.1 = (f32[128,896]{1,0:T(8,128)}, bf16[2,4,4,4,16,1024]{5,4,3,2,1,0:T(8,128)(2,1)}, f32[3,56,608]{2,1,0:T(8,128)}) custom-call(f32[128,896]{1,0:T(8,128)} %copy-done.2, f32[128,896]{1,0:T(8,128)} %copy-done.6, f32[128,896]{1,0:T(8,128)} %get-tuple-element.69.mid_ref, f32[128,896]{1,0:T(8,128)} %get-tuple-element.61.refs_0_.x_ref, ...), custom_call_target="tpu_custom_call" | custom-call | tf_op jit(solution)/shard_map/attention_backward_1/pallas_call | solution.py:1122
  262.3 0.0 copy-start.3
  262.3 1.0 copy-done.3
  263.3 40.7 %mlp_backward_0.1 = (f32[128,896]{1,0:T(8,128)S(1)}, bf16[3,896,608]{2,1,0:T(8,128)(2,1)}, f32[16,1024]{1,0:T(8,128)S(1)}) custom-call(f32[128,896]{1,0:T(8,128)S(1)} %copy-done.3, bf16[3,896,608]{2,1,0:T(8,128)(2,1)} %bitcast.34, bf16[4,2,128,896]{3,2,1,0:T(8,128)(2,1)} %get-tuple-element.80.refs_2_, bf16[4,256,608]{2,1,0:T(8,128)(2,1)} %get-tuple-element.81.refs_3_, ...), custom_call_target="tpu_custom_call" | custom-call | tf_op jit(solution)/shard_map/mlp_backward_0/pallas_call | solution.py:717
  304.0 0.0 copy-start.5
  304.1 0.8 copy-done.5
  304.8 0.0 copy-start.8
  304.8 0.6 copy-done.8
  305.4 36.2 %attention_backward_0.1 = (f32[128,896]{1,0:T(8,128)}, bf16[2,4,4,4,16,1024]{5,4,3,2,1,0:T(8,128)(2,1)}, f32[3,56,608]{2,1,0:T(8,128)}) custom-call(f32[128,896]{1,0:T(8,128)} %get-tuple-element.78.refs_0_.g_ref, f32[128,896]{1,0:T(8,128)} %copy-done.5, f32[128,896]{1,0:T(8,128)} %get-tuple-element.85.mid_ref, f32[128,896]{1,0:T(8,128)} %bitcast_convert_fusion.refs_0_.x_ref, ...), custom_call_target="tpu_custom_call" | custom-call | tf_op jit(solution)/shard_map/attention_backward_0/pallas_call | solution.py:1122
  341.7 0.0 copy-start.1
  341.7 2.2 copy-done.1
  343.9 0.0 copy-start.12
  343.9 32.2 %last_sum.1.a_zero = f32[16,1024]{1,0:T(8,128)S(1)} custom-call(bf16[2,4,4,4,16,1024]{5,4,3,2,1,0:T(8,128)(2,1)S(1)} %copy-done.1), custom_call_target="tpu_custom_call" | custom-call | tf_op jit(solution)/shard_map/last_sum/pallas_call | solution.py:748
  376.1 0.0 copy-start.7
  376.1 0.6 copy-done.7
  376.7 2.1 assemble.1
  378.9 1.5 copy.43
  380.4 1.3 copy.44
  381.7 1.5 copy.45
  383.1 1.0 slice_bitcast_fusion
  384.1 0.7 pad_maximum_fusion.1
  384.9 0.0 copy-done.12
  384.9 0.8 copy.47
  (5 shorter events, 0.1 us)
Async XLA Ops:
  0.6 57.9 %copy-start.14 = (s32[16]{0:T(128)S(1)}, s32[16]{0:T(128)}, u32[]{:S(2)}) copy-start(s32[16]{0:T(128)} %param.15) | copy-start | bytes 196
  3.9 0.7 copy-start.9
  4.6 0.7 copy-start.10
  5.2 0.7 copy-start.11
  49.8 2.0 copy-start
  51.9 0.8 copy-start.4
  140.6 52.9 %copy-start.13 = (bf16[1,128,896]{2,1,0:T(8,128)(2,1)S(1)}, bf16[1,128,896]{2,1,0:T(8,128)(2,1)}, u32[]{:S(2)}) copy-start(bf16[1,128,896]{2,1,0:T(8,128)(2,1)} %param.14) | copy-start | bytes 688132
  193.6 28.9 %copy-start.2 = (f32[128,896]{1,0:T(8,128)}, f32[128,896]{1,0:T(8,128)S(1)}, u32[]{:S(2)}) copy-start(f32[128,896]{1,0:T(8,128)S(1)} %bitcast_convert_fusion.1.refs_0_.g_ref) | copy-start | bytes 1376260
  222.5 0.8 copy-start.6
  262.3 1.0 copy-start.3
  304.0 0.8 copy-start.5
  304.8 0.6 copy-start.8
  341.7 2.2 copy-start.1
  343.9 41.0 %copy-start.12 = (f32[128,896]{1,0:T(8,128)S(1)}, f32[128,896]{1,0:T(8,128)}, u32[]{:S(2)}) copy-start(f32[128,896]{1,0:T(8,128)} %get-tuple-element.94) | copy-start | bytes 1376260
  376.1 0.6 copy-start.7
where the time goes:
time: 391 us; the launch traced here: 386 us
  Pallas kernels  356 us (91%)
  local copies, waits for them, and re-layouts  21.9 us (6%)
  other arithmetic  7.17 us (2%)
    pallas_call x2, Pallas kernels, forward(): pl.pallas_call(functools.partial(forward_kernel, layer), out_shape=tuple(...  133 us
    pallas_call x2, Pallas kernels, attention_backward(): pl.pallas_call(attention_backward_kernel, out_shape=(jax.ShapeDtypeStruct...  75.2 us
    pallas_call x2, Pallas kernels, mlp_backward(): pl.pallas_call(functools.partial(mlp_backward_kernel, layer, carries), ou...  69.7 us
    pallas_call x1, Pallas kernels, first_gather(): pl.pallas_call(first_gather_kernel, out_shape=(jax.ShapeDtypeStruct((4, 4...  44 us
    pallas_call x1, Pallas kernels, last_sum(): pl.pallas_call(last_sum_kernel, out_shape=jax.ShapeDtypeStruct((16, 1024)...  32.2 us
    unnamed x36, local copies, waits for them, and re-layouts  17.3 us

commit v1 on v0

--- a/solution.py
+++ b/solution.py
@@ -90,136 +90,148 @@
             copy.wait_send()
 
 
-class LineGather:
-    slots = 9
-
-    def __init__(self, mail, base, spot, plane, full, local_sem):
-        self.mail, self.base, self.spot, self.plane, self.full = mail, base, spot, plane, full
-        y, c = spot[2:]
-        self.own = pltpu.make_async_copy(plane, self.part(y, c), local_sem)
-
-    def part(self, row, core, half=None):
-        lead = pl.ds(0, 4) if half is None else pl.ds(2 * half, 2)
-        return self.full.at[lead, pl.ds(0, 4), 2 * row + core]
-
-    def send(self, slot, src, dst, target):
-        self.mail.send(self.base + slot, src, dst, target)
-
-    def take(self, slot, dst, source):
-        self.mail.take(self.base + slot, dst, source)
-
-    def names(self):
-        y, c = self.spot[2:]
-        return (y, c, up1(y), down1(y), up2(y)) + tuple(ctx_peers(self.spot))
+class RowGather:
+    slots = 8
+
+    def __init__(self, mail, spot, block, along_x, along_z, local_sem):
+        self.mail, self.spot, self.block = mail, spot, block
+        self.along_x, self.along_z = along_x, along_z
+        self.cut, self.rest = along_x.shape[0], along_z.shape[0]
+        x, z = spot[:2]
+        self.sa, self.sb = pl.ds(0, self.cut), pl.ds(self.cut, self.rest)
+        self.own = [
+            pltpu.make_async_copy(block.at[self.sa], along_x.at[:, x], local_sem.at[0]),
+            pltpu.make_async_copy(block.at[self.sb], along_z.at[:, z], local_sem.at[1]),
+        ]
 
     def step_one(self):
-        y, c, yp, ym, y2, to_yp, to_ym, other = self.names()
-        self.send(0, self.plane, self.part(y, c), to_yp)
-        self.send(1, self.plane, self.part(y, c), to_ym)
-        self.send(2, self.plane, self.part(y, c), other)
-        self.own.start()
+        x, z = self.spot[:2]
+        to_xp, to_xm, to_zp, to_zm = ring_peers(self.spot)
+        for copy in self.own:
+            copy.start()
+        self.mail.send(0, self.block.at[self.sa], self.along_x.at[:, x], to_xp)
+        self.mail.send(1, self.block.at[self.sa], self.along_x.at[:, x], to_xm)
+        self.mail.send(4, self.block.at[self.sb], self.along_z.at[:, z], to_zp)
+        self.mail.send(5, self.block.at[self.sb], self.along_z.at[:, z], to_zm)
+
+    def relays(self):
+        x, z = self.spot[:2]
+        to_xp, to_xm, to_zp, to_zm = ring_peers(self.spot)
+        return (
+            (0, self.along_x, self.cut, x, to_xp, to_xm),
+            (4, self.along_z, self.rest, z, to_zp, to_zm),
+        )
 
     def step_two(self):
-        y, c, yp, ym, y2, to_yp, to_ym, other = self.names()
-        self.take(0, self.part(ym, c), to_ym)
-        self.send(3, self.part(ym, c, 0), self.part(ym, c, 0), to_yp)
-        self.send(4, self.part(ym, c), self.part(ym, c), other)
-        self.take(1, self.part(yp, c), to_yp)
-        self.send(5, self.part(yp, c, 1), self.part(yp, c, 1), to_ym)
-        self.send(6, self.part(yp, c), self.part(yp, c), other)
+        for base, ref, count, here, plus, minus in self.relays():
+            behind, front = down1(here), up1(here)
+            half = max(count // 2, 1)
+            self.mail.take(base, ref.at[:, behind], minus)
+            part = ref.at[pl.ds(0, half), behind]
+            self.mail.send(base + 2, part, part, plus)
+            self.mail.take(base + 1, ref.at[:, front], plus)
+            if count > 1:
+                part = ref.at[pl.ds(half, count - half), front]
+                self.mail.send(base + 3, part, part, minus)
 
     def step_three(self):
-        y, c, yp, ym, y2, to_yp, to_ym, other = self.names()
-        self.take(3, self.part(y2, c, 0), to_ym)
-        self.send(7, self.part(y2, c, 0), self.part(y2, c, 0), other)
-        self.take(5, self.part(y2, c, 1), to_yp)
-        self.send(8, self.part(y2, c, 1), self.part(y2, c, 1), other)
+        for base, ref, count, here, plus, minus in self.relays():
+            half = max(count // 2, 1)
+            self.mail.take(base + 2, ref.at[pl.ds(0, half), up2(here)], minus)
+            if count > 1:
+                self.mail.take(base + 3, ref.at[pl.ds(half, count - half), up2(here)], plus)
+        for copy in self.own:
+            copy.wait()
+
+
+class PlaneFill:
+    slots = 16
+
+    def __init__(self, mail, spot, along_x, along_z, full, local_sem, mirror=None):
+        self.mail, self.spot, self.full, self.mirror = mail, spot, full, mirror
+        self.along_x, self.along_z = along_x, along_z
+        self.cut, self.rest = along_x.shape[0], along_z.shape[0]
+        x, z, y, c = spot
+        self.other = device(x, z, y, 1 - c)
+        self.copies = [
+            pltpu.make_async_copy(along_x, full.at[self.first(z)], local_sem.at[0]),
+            pltpu.make_async_copy(along_z, full.at[self.second(x)], local_sem.at[1]),
+        ]
+
+    def first(self, z, half=None):
+        lead = pl.ds(0, self.cut) if half is None else pl.ds(half * (self.cut // 2), self.cut // 2)
+        return (lead, pl.ds(0, 4), z)
+
+    def second(self, x, half=None):
+        if half is None:
+            return (pl.ds(self.cut, self.rest), x, pl.ds(0, 4))
+        if self.rest == 1:
+            return (pl.ds(self.cut, 1), x, pl.ds(2 * half, 2))
+        return (pl.ds(self.cut + half * (self.rest // 2), self.rest // 2), x, pl.ds(0, 4))
+
+    def pass_on(self, slot, where, target):
+        self.mail.send(slot, self.full.at[where], self.full.at[where], target)
+
+    def share(self, slot, where, src=None):
+        if self.mirror is not None:
+            src = self.full.at[where] if src is None else src
+            self.mail.send(slot, src, self.full.at[where], self.other)
+
+    def step_one(self):
+        x, z = self.spot[:2]
+        to_xp, to_xm, to_zp, to_zm = ring_peers(self.spot)
+        self.mail.send(0, self.along_x, self.full.at[self.first(z)], to_zp)
+        self.mail.send(1, self.along_x, self.full.at[self.first(z)], to_zm)
+        self.mail.send(2, self.along_z, self.full.at[self.second(x)], to_xp)
+        self.mail.send(3, self.along_z, self.full.at[self.second(x)], to_xm)
+        self.share(8, self.first(z), self.along_x)
+        self.share(9, self.second(x), self.along_z)
+        for copy in self.copies:
+            copy.start()
+
+    def step_two(self):
+        x, z = self.spot[:2]
+        to_xp, to_xm, to_zp, to_zm = ring_peers(self.spot)
+        xp, xm, zp, zm = up1(x), down1(x), up1(z), down1(z)
+        for slot, where, piece, source, target in (
+            (0, self.first(zm), self.first(zm, 0), to_zm, to_zp),
+            (2, self.second(xm), self.second(xm, 0), to_xm, to_xp),
+            (1, self.first(zp), self.first(zp, 1), to_zp, to_zm),
+            (3, self.second(xp), self.second(xp, 1), to_xp, to_xm),
+        ):
+            self.mail.take(slot, self.full.at[where], source)
+            self.pass_on(4 + slot, piece, target)
+            self.share(10 + slot, where)
+
+    def step_three(self):
+        x, z = self.spot[:2]
+        to_xp, to_xm, to_zp, to_zm = ring_peers(self.spot)
+        for slot, piece, source in (
+            (4, self.first(up2(z), 0), to_zm),
+            (6, self.second(up2(x), 0), to_xm),
+            (5, self.first(up2(z), 1), to_zp),
+            (7, self.second(up2(x), 1), to_xp),
+        ):
+            self.mail.take(slot, self.full.at[piece], source)
+        self.share(14, self.first(up2(z)))
+        self.share(15, self.second(up2(x)))
+        for copy in self.copies:
+            copy.wait()
 
     def step_four(self):
-        y, c, yp, ym, y2, to_yp, to_ym, other = self.names()
-        self.own.wait()
-        self.take(2, self.part(y, 1 - c), other)
-        self.take(4, self.part(ym, 1 - c), other)
-        self.take(6, self.part(yp, 1 - c), other)
-        self.take(7, self.part(y2, 1 - c, 0), other)
-        self.take(8, self.part(y2, 1 - c, 1), other)
-
-
-class PlaneGather:
-    slots = 15
-
-    def __init__(self, mail, base, spot, own, full, local_sem):
-        self.mail, self.base, self.spot, self.block, self.full = mail, base, spot, own, full
-        x, z = spot[:2]
-        self.own = pltpu.make_async_copy(own, full.at[:, x, z], local_sem)
-
-    def names(self):
-        x, z, y, c = self.spot
+        x, z = self.spot[:2]
         xp, xm, zp, zm = up1(x), down1(x), up1(z), down1(z)
-        to = (device(xp, z, y, c), device(xm, z, y, c), device(x, zp, y, c), device(x, zm, y, c))
-        return x, z, xp, xm, zp, zm, up2(x), up2(z), to
-
-    def pass_on(self, slot, where, target):
-        region = self.full.at[where]
-        self.mail.send(self.base + slot, region, region, target)
-
-    def take(self, slot, where, source):
-        self.mail.take(self.base + slot, self.full.at[where], source)
-
-    pair, one, two, three = pl.ds(0, 2), pl.ds(0, 1), pl.ds(1, 1), pl.ds(2, 1)
-    every, lo, hi = pl.ds(0, 4), pl.ds(0, 2), pl.ds(2, 2)
-
-    def step_one(self):
-        x, z, xp, xm, zp, zm, x2, z2, (to_xp, to_xm, to_zp, to_zm) = self.names()
-        self.own.start()
-        for slot, slabs, target in (
-            (0, self.pair, to_xp),
-            (1, self.pair, to_xm),
-            (2, self.three, to_zp),
-            (3, self.three, to_zm),
+        for slot, where in (
+            (8, self.first(z)),
+            (9, self.second(x)),
+            (10, self.first(zm)),
+            (11, self.first(zp)),
+            (12, self.second(xm)),
+            (13, self.second(xp)),
+            (14, self.first(up2(z))),
+            (15, self.second(up2(x))),
         ):
-            self.mail.send(
-                self.base + slot, self.block.at[slabs], self.full.at[slabs, x, z], target
-            )
-
-    def step_two(self):
-        x, z, xp, xm, zp, zm, x2, z2, (to_xp, to_xm, to_zp, to_zm) = self.names()
-        self.take(0, (self.pair, xm, z), to_xm)
-        self.pass_on(4, (self.one, xm, z), to_xp)
-        self.take(1, (self.pair, xp, z), to_xp)
-        self.pass_on(5, (self.two, xp, z), to_xm)
-        self.take(2, (self.three, x, zm), to_zm)
-        self.pass_on(6, (self.three, x, zm), to_zp)
-        self.take(3, (self.three, x, zp), to_zp)
-
-    def step_three(self):
-        x, z, xp, xm, zp, zm, x2, z2, (to_xp, to_xm, to_zp, to_zm) = self.names()
-        self.take(4, (self.one, x2, z), to_xm)
-        self.take(5, (self.two, x2, z), to_xp)
-        self.own.wait()
-        self.pass_on(7, (self.pair, self.every, z), to_zp)
-        self.pass_on(8, (self.pair, self.every, z), to_zm)
-        self.take(6, (self.three, x, z2), to_zm)
-        self.pass_on(9, (self.three, x, self.every), to_xp)
-        self.pass_on(10, (self.three, x, self.every), to_xm)
-
-    def step_four(self):
-        x, z, xp, xm, zp, zm, x2, z2, (to_xp, to_xm, to_zp, to_zm) = self.names()
-        self.take(7, (self.pair, self.every, zm), to_zm)
-        self.pass_on(11, (self.one, self.every, zm), to_zp)
-        self.take(8, (self.pair, self.every, zp), to_zp)
-        self.pass_on(12, (self.two, self.every, zp), to_zm)
-        self.take(9, (self.three, xm, self.every), to_xm)
-        self.pass_on(13, (self.three, xm, self.lo), to_xp)
-        self.take(10, (self.three, xp, self.every), to_xp)
-        self.pass_on(14, (self.three, xp, self.hi), to_xm)
-
-    def step_five(self):
-        x, z, xp, xm, zp, zm, x2, z2, (to_xp, to_xm, to_zp, to_zm) = self.names()
-        self.take(11, (self.one, self.every, z2), to_zm)
-        self.take(12, (self.two, self.every, z2), to_zp)
-        self.take(13, (self.three, x2, self.lo), to_xm)
-        self.take(14, (self.three, x2, self.hi), to_xp)
+            self.mail.take(slot, self.mirror.at[where], self.other)
 
 
 def ring_peers(spot):
@@ -238,9 +250,9 @@
 
 
 def first_gather_kernel(
-    one_ref, qkv_ref, bias_ref, out_ref, two_ref,
-    full, plane_out,
-    rows, vectors, offsets, plane, send_sem, recv_sem, local_sem,
+    one_ref, qkv_ref, bias_ref, out_ref, two_ref, m_ref,
+    full, row_out, m_x, m_z,
+    rows, vectors, offsets, line, a_x, a_z, send_sem, recv_sem, local_sem,
 ):
     spot = place()
     x, z, y, c = spot
@@ -261,68 +273,65 @@
         rows[l, 15:16, 0:D] = gains[2 + l : 3 + l, :D]
         rows[l, 7:8, D:1024] = bias[l : l + 1, :128]
         rows[l, 15:16, D:1024] = bias[l : l + 1, 128:]
-    plane[:, x, z] = rows[...].astype(BF)
-    xp, xm, zp, zm, x2, z2 = up1(x), down1(x), up1(z), down1(z), up2(x), up2(z)
-    to_xp, to_xm, to_zp, to_zm = ring_peers(spot)
-    greet(ring_peers(spot) + ctx_peers(spot))
-
-    def pass_on(slot, where, target):
-        mail.send(slot, plane.at[where], plane.at[where], target)
-
-    def take(slot, where, source):
-        mail.take(slot, plane.at[where], source)
-
-    both, every = pl.ds(0, 2), pl.ds(0, 4)
-    pass_on(0, (both, x, z), to_xp)
-    pass_on(1, (both, x, z), to_xm)
-    take(0, (both, xm, z), to_xm)
-    pass_on(2, (0, xm, z), to_xp)
-    take(1, (both, xp, z), to_xp)
-    pass_on(3, (1, xp, z), to_xm)
-    take(2, (0, x2, z), to_xm)
-    take(3, (1, x2, z), to_xp)
-    pass_on(4, (both, every, z), to_zp)
-    pass_on(5, (both, every, z), to_zm)
-    take(4, (both, every, zm), to_zm)
-    pass_on(6, (0, every, zm), to_zp)
-    take(5, (both, every, zp), to_zp)
-    pass_on(7, (1, every, zp), to_zm)
-    take(6, (0, every, z2), to_zm)
-    take(7, (1, every, z2), to_zp)
-    line = LineGather(mail, 8, spot, plane.at[0], full, local_sem.at[0])
-    line.step_one()
-    kept = pltpu.make_async_copy(plane.at[1], plane_out, local_sem.at[1])
+    line[:, y] = rows[...].astype(BF)
+    yp, ym, y2 = up1(y), down1(y), up2(y)
+    to_yp, to_ym, other = ctx_peers(spot)
+    to_y2 = device(x, z, y2, c)
+    greet(ring_peers(spot) + [to_yp, to_ym, other, to_y2])
+    mail.send(0, line.at[:, y], line.at[:, y], to_yp)
+    mail.send(1, line.at[:, y], line.at[:, y], to_ym)
+    mail.send(2, line.at[:, y], line.at[:, y], to_y2)
+    row = RowGather(mail.shifted(3), spot, line.at[0], a_x, a_z, local_sem.at[pl.ds(0, 2)])
+    fill = PlaneFill(
+        mail.shifted(11), spot, a_x, a_z, full.at[c], local_sem.at[pl.ds(2, 2)], full.at[1 - c]
+    )
+    feed = RowGather(mail.shifted(27), spot, m_ref.at[0], m_x, m_z, local_sem.at[pl.ds(4, 2)])
+    mail.take(0, line.at[:, ym], to_ym)
+    mail.take(1, line.at[:, yp], to_yp)
+    mail.take(2, line.at[:, y2], to_y2)
+    row.step_one()
+    kept = pltpu.make_async_copy(line.at[1], row_out, local_sem.at[6])
     kept.start()
-    line.step_two()
-    line.step_three()
-    line.step_four()
+    row.step_two()
+    row.step_three()
+    fill.step_one()
+    feed.step_one()
+    fill.step_two()
+    feed.step_two()
+    fill.step_three()
+    feed.step_three()
+    fill.step_four()
     kept.wait()
     mail.finish()
 
 
-def first_gather(gain_one, w_qkv, b_qkv, w_out, gain_two):
+def first_gather(gain_one, w_qkv, b_qkv, w_out, gain_two, m_block):
     return pl.pallas_call(
         first_gather_kernel,
         out_shape=(
-            jax.ShapeDtypeStruct((4, 4, 8, 16, 1024), BF),
-            jax.ShapeDtypeStruct((4, 4, 16, 1024), BF),
+            jax.ShapeDtypeStruct((2, 4, 4, 4, 16, 1024), BF),
+            jax.ShapeDtypeStruct((4, 16, 1024), BF),
+            jax.ShapeDtypeStruct((2, 4, 56, FS), BF),
+            jax.ShapeDtypeStruct((1, 4, 56, FS), BF),
         ),
-        in_specs=[pl.BlockSpec(memory_space=pltpu.VMEM)] * 5,
-        out_specs=[pl.BlockSpec(memory_space=pl.ANY)] * 2,
+        in_specs=[pl.BlockSpec(memory_space=pltpu.VMEM)] * 5 + [pl.BlockSpec(memory_space=pl.ANY)],
+        out_specs=[pl.BlockSpec(memory_space=pl.ANY)] * 4,
         scratch_shapes=[
             pltpu.VMEM((2, 16, 1024), F32),
             pltpu.VMEM((8, 1024), F32),
             pltpu.VMEM((8, 256), F32),
-            pltpu.VMEM((2, 4, 4, 16, 1024), BF),
-            pltpu.SemaphoreType.DMA((17,)),
-            pltpu.SemaphoreType.DMA((17,)),
-            pltpu.SemaphoreType.DMA((2,)),
+            pltpu.VMEM((2, 4, 16, 1024), BF),
+            pltpu.VMEM((2, 4, 16, 1024), BF),
+            pltpu.VMEM((2, 4, 16, 1024), BF),
+            pltpu.SemaphoreType.DMA((35,)),
+            pltpu.SemaphoreType.DMA((35,)),
+            pltpu.SemaphoreType.DMA((7,)),
         ],
         compiler_params=pltpu.CompilerParams(
             collective_id=1, has_side_effects=True, vmem_limit_bytes=16 * 1024 * 1024
         ),
         name="first_gather",
-    )(gain_one, w_qkv, b_qkv, w_out, gain_two)
+    )(gain_one, w_qkv, b_qkv, w_out, gain_two, m_block)
 
 
 class PlaneSum:
@@ -546,19 +555,24 @@
     x, z, y, c = spot
     yp, ym, y2 = up1(y), down1(y), up2(y)
     to_yp, to_ym, other = device(x, z, yp, c), device(x, z, ym, c), device(x, z, y, 1 - c)
+    begin, end = pl.ds(0, 32), pl.ds(32, 32)
     first, second = pl.ds(0, 64), pl.ds(64, 64)
-    mail.send(0, src, rows.at[y, c], to_yp)
-    mail.send(1, src, rows.at[y, c], to_ym)
+    mail.send(0, src.at[first], rows.at[y, c, first], to_yp)
+    mail.send(1, src.at[second], rows.at[y, c, second], to_ym)
     mail.send(2, src, rows.at[y, c], other)
+    mail.send(19, src.at[second], rows.at[y, c, second], to_yp)
+    mail.send(20, src.at[first], rows.at[y, c, first], to_ym)
     rows[y, c] = src[...]
     mail.take(2, rows.at[y, 1 - c], other)
     chunk(y)
     mail.send(12, part.at[y, 1 - c], near.at[3], other)
-    mail.take(0, rows.at[ym, c], to_ym)
+    mail.take(0, rows.at[ym, c, first], to_ym)
     mail.send(3, rows.at[ym, c, first], rows.at[ym, c, first], to_yp)
+    mail.take(1, rows.at[yp, c, second], to_yp)
+    mail.send(5, rows.at[yp, c, second], rows.at[yp, c, second], to_ym)
+    mail.take(19, rows.at[ym, c, second], to_ym)
     mail.send(4, rows.at[ym, c], rows.at[ym, c], other)
-    mail.take(1, rows.at[yp, c], to_yp)
-    mail.send(5, rows.at[yp, c, second], rows.at[yp, c, second], to_ym)
+    mail.take(20, rows.at[yp, c, first], to_yp)
     mail.send(6, rows.at[yp, c], rows.at[yp, c], other)
     mail.take(4, rows.at[ym, 1 - c], other)
     chunk(ym)
@@ -584,19 +598,27 @@
     fillers[0]()
     mail.take(9, near.at[0], other)
     own[0] = (part[y2, c].astype(F32) + near[0].astype(F32)).astype(BF)
-    mail.send(13, own.at[0, first], far.at[0], to_yp)
-    mail.send(14, own.at[0, second], far.at[1], to_ym)
+    mail.send(13, own.at[0, pl.ds(0, 32)], far.at[0, begin], to_yp)
+    mail.send(14, own.at[0, pl.ds(64, 32)], far.at[1, begin], to_ym)
+    mail.send(21, own.at[0, pl.ds(32, 32)], far.at[0, end], to_yp)
+    mail.send(22, own.at[0, pl.ds(96, 32)], far.at[1, end], to_ym)
     fillers[1]()
-    mail.take(13, far.at[0], to_ym)
-    mail.send(17, far.at[0], fin.at[0], to_yp)
-    mail.take(14, far.at[1], to_yp)
-    mail.send(18, far.at[1], fin.at[1], to_ym)
+    mail.take(13, far.at[0, begin], to_ym)
+    mail.send(17, far.at[0, begin], fin.at[0, begin], to_yp)
+    mail.take(14, far.at[1, begin], to_yp)
+    mail.send(18, far.at[1, begin], fin.at[1, begin], to_ym)
+    mail.take(21, far.at[0, end], to_ym)
+    mail.send(23, far.at[0, end], fin.at[0, end], to_yp)
+    mail.take(22, far.at[1, end], to_yp)
+    mail.send(24, far.at[1, end], fin.at[1, end], to_ym)
     fillers[2]()
     mail.take(12, near.at[3], other)
     mail.take(15, got.at[0], to_ym)
     mail.take(16, got.at[1], to_yp)
-    mail.take(17, fin.at[0], to_ym)
-    mail.take(18, fin.at[1], to_yp)
+    mail.take(17, fin.at[0, begin], to_ym)
+    mail.take(18, fin.at[1, begin], to_yp)
+    mail.take(23, fin.at[0, end], to_ym)
+    mail.take(24, fin.at[1, end], to_yp)
     total = (
         part[y, c].astype(F32)
         + near[3].astype(F32)
@@ -632,7 +654,7 @@
         )
     ]
     if carries:
-        older = AttentionSum(mail, 19, spot, before, refs[9:], local_sem.at[4])
+        older = AttentionSum(mail, 25, spot, before, refs[9:], local_sem.at[4])
         loads.append(older.load)
     for load in loads:
         load.start()
@@ -705,8 +727,8 @@
         pltpu.VMEM((4, 256, FS), BF),
         pltpu.VMEM((4, 256, FS), BF),
         pltpu.VMEM((128, D), BF),
-        pltpu.SemaphoreType.DMA((39,)),
-        pltpu.SemaphoreType.DMA((39,)),
+        pltpu.SemaphoreType.DMA((45,)),
+        pltpu.SemaphoreType.DMA((45,)),
         pltpu.SemaphoreType.DMA((5,)),
     ]
     operands = [grad_output, m_full, hidden_rows, gate, up]
@@ -780,7 +802,8 @@
     x_ref, a_ref, m_ref, pick_ref, cos_ref, sin_ref, qpos_ref, kpos_ref = refs[:8]
     refs = refs[8:]
     if layer == 0:
-        plane_ref, refs = refs[0], refs[1:]
+        row_ref, shard_ref, m_z_ref = refs[:3]
+        refs = refs[3:]
     out_ref, vec_ref, mid_ref, att_ref, qs_ref, kvs_ref, probs_ref, low_ref, high_ref = refs[:9]
     hr_ref, gate_ref, up_ref = refs[9:12]
     refs = refs[12:]
@@ -797,12 +820,23 @@
     load = pltpu.make_async_copy(a_ref, blocks, local_sem.at[0])
     load.start()
     if layer == 0:
-        line = LineGather(mail, 28, spot, plane_ref, a_one, local_sem.at[21])
-        now = PlaneGather(mail, 37, spot, m_ref.at[0], m_zero, local_sem.at[22])
-        later = PlaneGather(mail, 52, spot, m_ref.at[1], m_one, local_sem.at[23])
+        a_x, a_z, m_x, m_z, slabs = refs[6:]
+
+        def sems(k):
+            return local_sem.at[pl.ds(21 + 2 * k, 2)]
+
+        fill = PlaneFill(mail.shifted(34), spot, m_ref, m_z_ref, m_zero, sems(0))
+        a_row = RowGather(mail.shifted(50), spot, row_ref, a_x, a_z, sems(1))
+        m_row = RowGather(mail.shifted(58), spot, shard_ref.at[1], m_x, m_z, sems(2))
+        a_fill = PlaneFill(
+            mail.shifted(66), spot, a_x, a_z, a_one.at[c], sems(3), a_one.at[1 - c]
+        )
+        m_fill = PlaneFill(mail.shifted(82), spot, m_x, m_z, m_one, sems(4))
+        load_w = pltpu.make_async_copy(m_zero, slabs, local_sem.at[1])
         greet(ctx_peers(spot) + ring_peers(spot))
-        now.step_one()
-        line.step_one()
+        fill.step_one()
+        a_row.step_one()
+        m_row.step_one()
     else:
         load_w = pltpu.make_async_copy(m_ref, w, local_sem.at[1])
         load_w.start()
@@ -812,7 +846,9 @@
     load.wait()
     spare = []
     for g in range(8):
-        group = blocks[g // 2, 2 * (g % 2) : 2 * (g % 2) + 2].reshape(256, 1024)
+        group = jnp.concatenate(
+            [blocks[k % 2, k % 8 // 2, g // 2, 2 * (g % 2) + k // 8] for k in range(16)], axis=0
+        )
         low[112 * g : 112 * (g + 1)] = nn(pick_ref[0:112, :], group).astype(BF)
         high[112 * g : 112 * (g + 1)] = nn(pick_ref[112:224, :], group).astype(BF)
         spare.append(nn(pick_ref[224:240, :], group))
@@ -844,7 +880,8 @@
     for store in stores:
         store.start()
     if layer == 0:
-        now.step_two()
+        a_row.step_two()
+        m_row.step_two()
     for h in range(H):
         qs[h] = (turned[:, HD * h : HD * (h + 1)] * HD ** (-0.5)).astype(BF)
     mask[...] = jnp.where(kpos_ref[...] <= qpos_ref[...], 0.0, 1.0)
@@ -859,7 +896,9 @@
     mail.take(5, kv.at[y2, c, second], to_yp)
     mail.send(8, kv.at[y2, c, second], kv.at[y2, c, second], other)
     if layer == 0:
-        now.step_three()
+        fill.step_two()
+        a_row.step_three()
+        m_row.step_three()
     mail.take(2, kv.at[y, 1 - c], other)
     mail.take(4, kv.at[ym, 1 - c], other)
     mail.take(6, kv.at[yp, 1 - c], other)
@@ -881,10 +920,8 @@
 
     lax.fori_loop(0, 4, body, 0)
     if layer == 0:
-        line.step_two()
+        a_fill.step_one()
     lax.fori_loop(4, 7, body, 0)
-    if layer == 0:
-        now.step_four()
     att[...] = jnp.concatenate([heads[h] for h in range(H)], axis=1)
     mid[...] = inputs + nn(att[...], high[:, 128:])
     h2[...] = (normal(mid[...])[0] * gains[1:2]).astype(BF)
@@ -894,12 +931,9 @@
         stores.append(pltpu.make_async_copy(src, dst, local_sem.at[4 + i]))
         stores[-1].start()
     if layer == 0:
-        line.step_three()
-        now.step_five()
-        slabs = refs[6]
-        load_w = pltpu.make_async_copy(m_zero, slabs, local_sem.at[1])
+        fill.step_three()
         load_w.start()
-        later.step_one()
+        m_fill.step_one()
 
     loaded = []
 
@@ -926,18 +960,17 @@
 
     steps = [nothing] * 4
     if layer == 0:
-        steps = [later.step_two, later.step_three, later.step_four, nothing]
+        steps = [a_fill.step_two, a_fill.step_three, m_fill.step_two, m_fill.step_three]
     total = mlp_exchange(mail.shifted(9), spot, h2, buffers, chunk, steps[1:], steps[0])
     out_ref[...] = mid[...] + total
     if layer == 0:
-        later.step_five()
-        line.step_four()
+        a_fill.step_four()
     for store in stores:
         store.wait()
     mail.finish()
 
 
-def forward(layer, state, a_full, m_full, pick, tables, positions, plane):
+def forward(layer, state, a_full, m_full, pick, tables, positions, *shards):
     anywhere = pl.BlockSpec(memory_space=pl.ANY)
     vmem = pl.BlockSpec(memory_space=pltpu.VMEM)
     out_shape = [
@@ -956,24 +989,31 @@
     ]
     operands = [state, a_full, m_full, pick, *tables, *positions]
     in_specs = [vmem, anywhere, anywhere] + [vmem] * 5
-    slots = 28
+    slots = 34
+    extra = []
     if layer == 0:
         out_shape += [
             jax.ShapeDtypeStruct((3, 4, 4, 56, FS), BF),
             jax.ShapeDtypeStruct((3, 4, 4, 56, FS), BF),
-            jax.ShapeDtypeStruct((4, 4, 8, 16, 1024), BF),
+            jax.ShapeDtypeStruct((2, 4, 4, 4, 16, 1024), BF),
         ]
-        operands.append(plane)
-        in_specs.append(anywhere)
-        slots = 67
-    slabs = [pltpu.VMEM((3, 4, 4, 56, FS), BF)] if layer == 0 else []
+        operands += shards
+        in_specs += [anywhere] * 3
+        slots = 98
+        extra = [
+            pltpu.VMEM((2, 4, 16, 1024), BF),
+            pltpu.VMEM((2, 4, 16, 1024), BF),
+            pltpu.VMEM((2, 4, 56, FS), BF),
+            pltpu.VMEM((1, 4, 56, FS), BF),
+            pltpu.VMEM((3, 4, 4, 56, FS), BF),
+        ]
     return pl.pallas_call(
         functools.partial(forward_kernel, layer),
         out_shape=tuple(out_shape),
         in_specs=in_specs,
         out_specs=[vmem] * 2 + [anywhere] * (len(out_shape) - 2),
         scratch_shapes=[
-            pltpu.VMEM((4, 4, 8, 16, 1024), BF),
+            pltpu.VMEM((2, 4, 4, 4, 16, 1024), BF),
             pltpu.VMEM((D, 1024), BF),
             pltpu.VMEM((D, 1024), BF),
             pltpu.VMEM((4, 2, 128, 256), BF),
@@ -993,9 +1033,9 @@
             pltpu.VMEM((4, 256, FS), BF),
             pltpu.SemaphoreType.DMA((slots,)),
             pltpu.SemaphoreType.DMA((slots,)),
-            pltpu.SemaphoreType.DMA((24,)),
+            pltpu.SemaphoreType.DMA((31,)),
         ]
-        + slabs,
+        + extra,
         compiler_params=pltpu.CompilerParams(
             collective_id=12 + layer, has_side_effects=True, vmem_limit_bytes=56 * 1024 * 1024
         ),
@@ -1225,13 +1265,13 @@
     spread = jnp.asarray(spread, BF)
 
     m_block = jnp.stack([w_gate, w_up, w_down.transpose(0, 2, 1)], axis=1)
-    a_zero, plane_one = first_gather(gain_one, w_qkv, b_qkv, w_out, gain_two)
+    a_zero, row_one, m_x, m_z = first_gather(gain_one, w_qkv, b_qkv, w_out, gain_two, m_block)
     state_zero = tokens.reshape(local_len, width).astype(F32)
     state_one, *saved_zero, m_zero, m_one, a_one = forward(
-        0, state_zero, a_zero, m_block, pick, tables, positions, plane_one
+        0, state_zero, a_zero, m_x, pick, tables, positions, row_one, m_block, m_z
     )
     m_full = (m_zero.reshape(3, D, FS), m_one.reshape(3, D, FS))
-    state, *saved_one = forward(1, state_one, a_one, m_full[1], pick, tables, positions, None)
+    state, *saved_one = forward(1, state_one, a_one, m_full[1], pick, tables, positions)
     vectors = (saved_zero[0], saved_one[0])
     kept_layers = [
         ((state_zero,) + tuple(saved_zero[1:8]), saved_zero[8:]),

time: 391 us -> 367 us (0.939)
  Pallas kernels: 356 us -> 331 us
    pallas_call x2, Pallas kernels: 133 us -> 117 us  [forward(): pl.pallas_call(functools.partial(forward_kernel, layer), out_shape=tuple(...]
    pallas_call x1, Pallas kernels: 44 us -> 34.5 us  [first_gather(): pl.pallas_call(first_gather_kernel, out_shape=(jax.ShapeDtypeStruct((2, 4...]
    unnamed x36 -> x42, local copies, waits for them, and re-layouts: 17.3 us -> 18.7 us
where the time goes in v1:
time: 367 us; the launch traced here: 362 us
  Pallas kernels  331 us (90%)
  local copies, waits for them, and re-layouts  23.4 us (6%)
  other arithmetic  6.41 us (2%)
    pallas_call x2, Pallas kernels, forward(): pl.pallas_call(functools.partial(forward_kernel, layer), out_shape=tuple(...  117 us
    pallas_call x2, Pallas kernels, attention_backward(): pl.pallas_call(attention_backward_kernel, out_shape=(jax.ShapeDtypeStruct...  74.8 us
    pallas_call x2, Pallas kernels, mlp_backward(): pl.pallas_call(functools.partial(mlp_backward_kernel, layer, carries), ou...  70.6 us
    pallas_call x1, Pallas kernels, first_gather(): pl.pallas_call(first_gather_kernel, out_shape=(jax.ShapeDtypeStruct((2, 4...  34.5 us
    pallas_call x1, Pallas kernels, last_sum(): pl.pallas_call(last_sum_kernel, out_shape=jax.ShapeDtypeStruct((16, 1024)...  31.1 us
    unnamed x42, local copies, waits for them, and re-layouts  18.7 us

profile of v1, /device:TPU:0, one launch (start us, length us, event | category | flops | bytes accessed | tf_op | source)
XLA Modules:
  0.0 361.7 jit_solution(3830295225764868387)
XLA Ops:
  0.6 0.0 copy-start.17
  0.7 1.7 bitcast_convert_fusion.refs_0_.x_ref
  2.4 0.8 copy.31.qkv_ref
  3.2 0.7 copy.32.out_ref
  3.9 1.1 pad_maximum_fusion.m_ref.refs_9_
  5.0 0.0 copy-start.12
  5.0 0.6 copy-done.12
  5.7 0.0 copy-start.13
  5.7 0.7 copy-done.13
  6.3 0.0 copy-start.14
  6.3 0.7 copy-done.14
  7.0 0.0 copy-start.3
  7.0 34.5 %first_gather.1 = (bf16[2,4,4,4,16,1024]{5,4,3,2,1,0:T(8,128)(2,1)S(1)}, bf16[4,16,1024]{2,1,0:T(8,128)(2,1)S(1)}, bf16[2,4,56,608]{3,2,1,0:T(8,128)(2,1)S(1)}, bf16[1,4,56,608]{3,2,1,0:T(8,128)(2,1)S(1)}) custom-call(bf16[2,7]{1,0:T(2,128)(2,1)S(1)} %copy-done.12, bf16[2,7,1152]{2,1,0:T(8,128)(2,1)S(1)} %copy.31.qkv_ref, bf16[2,9]{1,0:T(2,128)(2,1)S(1)} %copy-done.13, ...), custom_call_target="tpu_custom_call" | custom-call | tf_op jit(solution)/shard_map/first_gather/pallas_call | solution.py:309
  41.6 0.0 copy-start
  41.6 2.1 copy-done
  43.6 0.0 copy-start.5
  43.6 0.8 copy-done.5
  44.4 0.0 copy-start.8
  44.4 0.7 copy-done.8
  45.1 0.0 copy-start.10
  45.1 0.7 copy-done.10
  45.8 0.7 dynamic-slice_multiply_fusion
  46.5 0.1 iota_add_fusion.1
  46.6 0.1 convert_element_type.26
  46.7 0.1 fusion
  46.8 0.1 tile.8
  46.9 1.0 copy.33.refs_4_.cos_ref
  48.0 1.0 copy.34.refs_5_.sin_ref
  49.0 0.8 add.63.refs_6_
  49.8 0.0 copy-done.17
  49.8 0.1 iota_add_fusion
  49.8 0.7 add.62.refs_7_
  50.5 0.0 copy-done.3
  50.5 66.7 %forward_layer_0.1 = (f32[128,896]{1,0:T(8,128)}, f32[8,1152]{1,0:T(8,128)}, f32[128,896]{1,0:T(8,128)}, bf16[128,896]{1,0:T(8,128)(2,1)}, bf16[14,128,64]{2,1,0...) custom-call(f32[128,896]{1,0:T(8,128)} %bitcast_convert_fusion.refs_, ...), custom_call_target="tpu_custom_call" | custom-call | tf_op jit(solution)/shard_map/forward_layer_0/pallas_call | solution.py:1010
  117.2 0.0 copy-start.16
  117.2 50.7 %forward_layer_1.1 = (f32[128,896]{1,0:T(8,128)}, f32[8,1152]{1,0:T(8,128)}, f32[128,896]{1,0:T(8,128)}, bf16[128,896]{1,0:T(8,128)(2,1)}, bf16[14,128,64]{2,1,0...) custom-call(f32[128,896]{1,0:T(8,128)} %get-tuple-element.65.refs_0_, ...), custom_call_target="tpu_custom_call" | custom-call | tf_op jit(solution)/shard_map/forward_layer_1/pallas_call | solution.py:1010
  167.9 1.7 convert_bitcast_fusion
  169.7 0.0 copy-done.16
  169.7 0.0 copy-start.2
  169.7 30.0 %mlp_backward_1.1 = (f32[128,896]{1,0:T(8,128)S(1)}, bf16[3,896,608]{2,1,0:T(8,128)(2,1)}) custom-call(f32[128,896]{1,0:T(8,128)S(1)} %bitcast_convert_fusion.1.refs_0_.g_ref, bf16[3,896,608]{2,1,0:T(8,128)(2,1)} %bitcast.33, bf16[4,2,128,896]{3,2,1,0:T(8,128)(2,1)} %get-tuple-element.69.refs_2_, bf16[4,256,608]{2,1,0:T(8,128)(2,1)} %get-tuple-element.70.refs_3_, ...), custom_call_target="tpu_custom_call" | custom-call | tf_op jit(solution)/shard_map/mlp_backward_1/pallas_call | solution.py:739
  199.7 0.0 copy-done.2
  199.7 0.0 copy-start.7
  199.7 0.8 copy-done.7
  200.5 36.9 %attention_backward_1.1 = (f32[128,896]{1,0:T(8,128)}, bf16[2,4,4,4,16,1024]{5,4,3,2,1,0:T(8,128)(2,1)}, f32[3,56,608]{2,1,0:T(8,128)}) custom-call(f32[128,896]{1,0:T(8,128)} %copy-done.2, f32[128,896]{1,0:T(8,128)} %copy-done.7, f32[128,896]{1,0:T(8,128)} %get-tuple-element.73.mid_ref, f32[128,896]{1,0:T(8,128)} %get-tuple-element.65.refs_0_.x_ref, ...), custom_call_target="tpu_custom_call" | custom-call | tf_op jit(solution)/shard_map/attention_backward_1/pallas_call | solution.py:1162
  237.4 0.0 copy-start.4
  237.5 1.0 copy-done.4
  238.5 40.6 %mlp_backward_0.1 = (f32[128,896]{1,0:T(8,128)S(1)}, bf16[3,896,608]{2,1,0:T(8,128)(2,1)}, f32[16,1024]{1,0:T(8,128)S(1)}) custom-call(f32[128,896]{1,0:T(8,128)S(1)} %copy-done.4, bf16[3,896,608]{2,1,0:T(8,128)(2,1)} %bitcast.34, bf16[4,2,128,896]{3,2,1,0:T(8,128)(2,1)} %get-tuple-element.84.refs_2_, bf16[4,256,608]{2,1,0:T(8,128)(2,1)} %get-tuple-element.85.refs_3_, ...), custom_call_target="tpu_custom_call" | custom-call | tf_op jit(solution)/shard_map/mlp_backward_0/pallas_call | solution.py:739
  279.1 0.0 copy-start.6
  279.1 0.8 copy-done.6
  279.8 0.6 copy-done.11
  280.5 37.9 %attention_backward_0.1 = (f32[128,896]{1,0:T(8,128)}, bf16[2,4,4,4,16,1024]{5,4,3,2,1,0:T(8,128)(2,1)}, f32[3,56,608]{2,1,0:T(8,128)}) custom-call(f32[128,896]{1,0:T(8,128)} %get-tuple-element.82.refs_0_.g_ref, f32[128,896]{1,0:T(8,128)} %copy-done.6, f32[128,896]{1,0:T(8,128)} %get-tuple-element.89.mid_ref, f32[128,896]{1,0:T(8,128)} %bitcast_convert_fusion.refs_0_.x_ref, ...), custom_call_target="tpu_custom_call" | custom-call | tf_op jit(solution)/shard_map/attention_backward_0/pallas_call | solution.py:1162
  318.4 0.0 copy-start.1
  318.4 2.2 copy-done.1
  320.6 31.1 %last_sum.1.a_zero = f32[16,1024]{1,0:T(8,128)S(1)} custom-call(bf16[2,4,4,4,16,1024]{5,4,3,2,1,0:T(8,128)(2,1)S(1)} %copy-done.1), custom_call_target="tpu_custom_call" | custom-call | tf_op jit(solution)/shard_map/last_sum/pallas_call | solution.py:770
  351.7 0.0 copy-start.9
  351.7 0.6 copy-done.9
  352.3 2.1 assemble.1
  354.5 1.5 copy.43
  356.0 1.3 copy.44
  357.3 1.5 copy.45
  358.7 1.0 slice_bitcast_fusion
  359.7 0.7 pad_maximum_fusion.1
  360.5 0.0 copy-done.15
  360.5 0.8 copy.47
  (7 shorter events, 0.1 us)
Async XLA Ops:
  0.6 49.1 %copy-start.17 = (s32[16]{0:T(128)S(1)}, s32[16]{0:T(128)}, u32[]{:S(2)}) copy-start(s32[16]{0:T(128)} %param.15) | copy-start | bytes 196
  5.0 0.7 copy-start.12
  5.7 0.7 copy-start.13
  6.3 0.7 copy-start.14
  7.0 43.5 %copy-start.3 = (bf16[2,3,56,608]{3,2,1,0:T(8,128)(2,1)}, bf16[2,3,56,608]{3,2,1,0:T(8,128)(2,1)S(1)}, u32[]{:S(2)}) copy-start(bf16[2,3,56,608]{3,2,1,0:T(8,128)(2,1)S(1)} %pad_maximum_fusion.m_ref.refs_9_) | copy-start | bytes 1225732
  41.6 2.1 copy-start
  43.6 0.8 copy-start.5
  44.4 0.7 copy-start.8
  45.1 0.7 copy-start.10
  117.2 52.5 %copy-start.16 = (bf16[1,128,896]{2,1,0:T(8,128)(2,1)S(1)}, bf16[1,128,896]{2,1,0:T(8,128)(2,1)}, u32[]{:S(2)}) copy-start(bf16[1,128,896]{2,1,0:T(8,128)(2,1)} %param.14) | copy-start | bytes 688132
  169.7 30.0 %copy-start.2 = (f32[128,896]{1,0:T(8,128)}, f32[128,896]{1,0:T(8,128)S(1)}, u32[]{:S(2)}) copy-start(f32[128,896]{1,0:T(8,128)S(1)} %bitcast_convert_fusion.1.refs_0_.g_ref) | copy-start | bytes 1376260
  199.7 0.8 copy-start.7
  237.4 1.0 copy-start.4
  279.1 0.8 copy-start.6
  279.8 0.6 copy-start.11
  318.4 2.2 copy-start.1
  320.6 39.9 %copy-start.15 = (f32[128,896]{1,0:T(8,128)S(1)}, f32[128,896]{1,0:T(8,128)}, u32[]{:S(2)}) copy-start(f32[128,896]{1,0:T(8,128)} %get-tuple-element.98) | copy-start | bytes 1376260
  351.7 0.6 copy-start.9

commit v2 on v1

--- a/solution.py
+++ b/solution.py
@@ -374,7 +374,8 @@
         self.mail.take(self.base + slot, dst, source)
 
     def add(self, where, extra):
-        self.g[where] = (self.g[where].astype(F32) + extra.astype(F32)).astype(BF)
+        part = self.g.at[where]
+        part[...] = (part[...].astype(F32) + extra.astype(F32)).astype(BF)
 
     def step_one(self):
         x, z, xp, xm, zp, zm, x2, z2, (to_xp, to_xm, to_zp, to_zm) = self.names()
@@ -455,11 +456,11 @@
         self.take(12, qa.at[0], to_xm)
         self.take(13, qa.at[1], to_xp)
         out[sa] = (
-            self.g[sa, x, z].astype(F32) + qa[0].astype(F32) + qa[1].astype(F32)
+            self.g.at[sa, x, z][...].astype(F32) + qa[0].astype(F32) + qa[1].astype(F32)
         ).astype(out.dtype)
         self.take(14, qb.at[0], to_zm)
         self.take(15, qb.at[1], to_zp)
-        total = self.g[sb, x, z].astype(F32) + qb[0].astype(F32) + qb[1].astype(F32)
+        total = self.g.at[sb, x, z][...].astype(F32) + qb[0].astype(F32) + qb[1].astype(F32)
         if rest == 1:
             self.take(10, pb.at[0], device(x, z2, y, c))
             total = total + pb[0].astype(F32)
@@ -467,47 +468,31 @@
 
 
 class AttentionSum:
-    def __init__(self, mail, base, spot, a_ref, refs, load_sem):
-        self.mail, self.base, self.spot, self.a_ref = mail, base, spot, a_ref
-        self.mine, self.near, self.block, self.got = refs[:4]
-        self.plane = PlaneSum(mail, base + 4, spot, self.mine, 2, refs[4:])
-        self.load = pltpu.make_async_copy(a_ref.at[spot[3]], self.mine, load_sem)
+    slots = 23
+
+    def __init__(self, mail, spot, mine, theirs, refs):
+        self.mail, self.spot, self.mine, self.theirs = mail, spot, mine, theirs
+        self.near, self.block, self.got = refs[:3]
+        self.plane = PlaneSum(mail, 7, spot, mine, 2, refs[3:])
 
     @staticmethod
     def scratch():
         return [
             pltpu.VMEM((4, 4, 4, 16, 1024), BF),
-            pltpu.VMEM((4, 4, 4, 16, 1024), BF),
             pltpu.VMEM((4, 16, 1024), BF),
             pltpu.VMEM((3, 16, 1024), BF),
         ] + PlaneSum.scratch(4, 2, 16, 1024)
 
-    slots = 20
-
-    @staticmethod
-    def peers(spot):
-        x, z, y, c = spot
-        return PlaneSum.peers(spot, 4, 2) + [
-            device(x, z, up1(y), c),
-            device(x, z, up2(y), c),
-            device(x, z, down1(y), c),
-            device(x, z, y, 1 - c),
-        ]
-
-    def start(self):
+    def start(self, i):
         x, z, y, c = self.spot
-        self.mail.send(self.base, self.a_ref.at[1 - c], self.near, device(x, z, y, 1 - c))
+        self.mail.send(i, self.theirs.at[:, i], self.near.at[:, i], device(x, z, y, 1 - c))
 
     def cores(self):
         x, z, y, c = self.spot
-        self.load.wait()
-        self.mail.take(self.base, self.near, device(x, z, y, 1 - c))
-
-        def body(i, carry):
-            self.mine[i] = (self.mine[i].astype(F32) + self.near[i].astype(F32)).astype(BF)
-            return carry
-
-        lax.fori_loop(0, 4, body, 0)
+        for i in range(4):
+            self.mail.take(i, self.near.at[:, i], device(x, z, y, 1 - c))
+            part = self.mine.at[:, i]
+            part[...] = (part[...].astype(F32) + self.near[:, i].astype(F32)).astype(BF)
         self.plane.step_one()
 
     def rows(self):
@@ -515,13 +500,13 @@
         self.plane.step_five(self.block)
         for k, step in enumerate((up1, up2, down1)):
             to = device(x, z, step(y), c)
-            self.mail.send(self.base + 1 + k, self.block.at[step(y)], self.got.at[k], to)
+            self.mail.send(4 + k, self.block.at[step(y)], self.got.at[k], to)
 
     def last(self, out):
         x, z, y, c = self.spot
         total = self.block[y].astype(F32)
         for k, step in enumerate((down1, up2, up1)):
-            self.mail.take(self.base + 1 + k, self.got.at[k], device(x, z, step(y), c))
+            self.mail.take(4 + k, self.got.at[k], device(x, z, step(y), c))
             total = total + self.got[k].astype(F32)
         out[...] = total
 
@@ -632,159 +617,6 @@
     return None
 
 
-def mlp_backward_kernel(layer, carries, *refs):
-    g_ref, w_ref, hr_ref, gate_ref, up_ref = refs[:5]
-    refs = refs[5:]
-    if carries:
-        before, refs = refs[0], refs[1:]
-    out_ref, grads = refs[:2]
-    refs = refs[2:]
-    if carries:
-        summed, refs = refs[0], refs[1:]
-    buffers, refs = refs[:7], refs[7:]
-    w, hr, gate, up, act, src, send_sem, recv_sem, local_sem = refs[:9]
-    rows, part = buffers[0], buffers[1]
-    spot = place()
-    x, z, y, c = spot
-    mail = Mail(send_sem, recv_sem)
-    loads = [
-        pltpu.make_async_copy(a, b, local_sem.at[i])
-        for i, (a, b) in enumerate(
-            ((w_ref, w), (gate_ref, gate), (up_ref, up), (hr_ref, hr))
-        )
-    ]
-    if carries:
-        older = AttentionSum(mail, 25, spot, before, refs[9:], local_sem.at[4])
-        loads.append(older.load)
-    for load in loads:
-        load.start()
-    src[...] = g_ref[...].astype(BF)
-    greet(AttentionSum.peers(spot) if carries else ctx_peers(spot))
-    loaded = []
-
-    def chunk(row):
-        if not loaded:
-            for load in loads[:3]:
-                load.wait()
-            loaded.append(True)
-        gz = rows[row].reshape(256, D)
-        gact = nn(gz, w[2])
-        g = gate[row].astype(F32)
-        u = up[row].astype(F32)
-        s = 1.0 / (1.0 + jnp.exp(-g))
-        silu = g * s
-        act[row] = (silu * u).astype(BF)
-        gg = (gact * u * (s + silu * (1.0 - s))).astype(BF)
-        gu = (gact * silu).astype(BF)
-        gate[row] = gg
-        up[row] = gu
-        part[row] = (nt(gg, w[0]) + nt(gu, w[1])).astype(BF).reshape(2, 128, D)
-
-    def weight_grad(member, left, right):
-        def run():
-            r = right[...].reshape(1024, FS)
-            for i in range(7):
-                l = left[:, :, :, 128 * i : 128 * (i + 1)].reshape(1024, 128)
-                grads[member, 128 * i : 128 * (i + 1)] = tn(l, r).astype(BF)
-
-        return run
-
-    def gates():
-        loads[3].wait()
-        weight_grad(0, hr, gate)()
-
-    fillers = [weight_grad(2, rows, act), gates, weight_grad(1, hr, up)]
-    hook = nothing
-    if carries:
-        older.start()
-        hook = older.cores
-        steps = [older.plane.step_two, older.plane.step_three, older.plane.step_four]
-
-        def joined(step, filler):
-            def run():
-                step()
-                filler()
-
-            return run
-
-        fillers = [joined(step, filler) for step, filler in zip(steps, fillers)]
-    out_ref[...] = mlp_exchange(mail, spot, src, buffers, chunk, fillers, hook)
-    if carries:
-        older.rows()
-        older.last(summed)
-    mail.finish()
-
-
-def mlp_backward(layer, grad_output, m_full, hidden_rows, gate, up, before):
-    anywhere = pl.BlockSpec(memory_space=pl.ANY)
-    vmem = pl.BlockSpec(memory_space=pltpu.VMEM)
-    carries = before is not None
-    out_shape = [jax.ShapeDtypeStruct((128, D), F32), jax.ShapeDtypeStruct((3, D, FS), BF)]
-    scratch = mlp_scratch() + [
-        pltpu.VMEM((3, D, FS), BF),
-        pltpu.VMEM((4, 2, 128, D), BF),
-        pltpu.VMEM((4, 256, FS), BF),
-        pltpu.VMEM((4, 256, FS), BF),
-        pltpu.VMEM((4, 256, FS), BF),
-        pltpu.VMEM((128, D), BF),
-        pltpu.SemaphoreType.DMA((45,)),
-        pltpu.SemaphoreType.DMA((45,)),
-        pltpu.SemaphoreType.DMA((5,)),
-    ]
-    operands = [grad_output, m_full, hidden_rows, gate, up]
-    if carries:
-        out_shape.append(jax.ShapeDtypeStruct((16, 1024), F32))
-        scratch += AttentionSum.scratch()
-        operands.append(before)
-    return pl.pallas_call(
-        functools.partial(mlp_backward_kernel, layer, carries),
-        out_shape=tuple(out_shape),
-        in_specs=[vmem] + [anywhere] * (len(operands) - 1),
-        out_specs=[vmem] * len(out_shape),
-        scratch_shapes=scratch,
-        compiler_params=pltpu.CompilerParams(
-            collective_id=10 + layer, has_side_effects=True, vmem_limit_bytes=52 * 1024 * 1024
-        ),
-        name="mlp_backward_%d" % layer,
-    )(*operands)
-
-
-def last_sum_kernel(a_ref, out_ref, *refs):
-    send_sem, recv_sem, local_sem = refs[-3:]
-    spot = place()
-    mail = Mail(send_sem, recv_sem)
-    older = AttentionSum(mail, 0, spot, a_ref, refs[:-3], local_sem.at[0])
-    older.load.start()
-    greet(AttentionSum.peers(spot))
-    older.start()
-    older.cores()
-    older.plane.step_two()
-    older.plane.step_three()
-    older.plane.step_four()
-    older.rows()
-    older.last(out_ref)
-    mail.finish()
-
-
-def last_sum(a_grads):
-    return pl.pallas_call(
-        last_sum_kernel,
-        out_shape=jax.ShapeDtypeStruct((16, 1024), F32),
-        in_specs=[pl.BlockSpec(memory_space=pl.ANY)],
-        out_specs=pl.BlockSpec(memory_space=pltpu.VMEM),
-        scratch_shapes=AttentionSum.scratch()
-        + [
-            pltpu.SemaphoreType.DMA((20,)),
-            pltpu.SemaphoreType.DMA((20,)),
-            pltpu.SemaphoreType.DMA((1,)),
-        ],
-        compiler_params=pltpu.CompilerParams(
-            collective_id=2, has_side_effects=True, vmem_limit_bytes=32 * 1024 * 1024
-        ),
-        name="last_sum",
-    )(a_grads)
-
-
 def swap_halves(u):
     width = u.shape[1]
     lane = lax.broadcasted_iota(jnp.int32, u.shape, 1)
@@ -841,7 +673,7 @@
         load_w = pltpu.make_async_copy(m_ref, w, local_sem.at[1])
         load_w.start()
         greet(ctx_peers(spot))
-    inputs = x_ref[...]
+    inputs = x_ref[...].astype(F32)
     n, r = normal(inputs)
     load.wait()
     spare = []
@@ -868,7 +700,9 @@
     hidden = (n * gains[0:1]).astype(BF)
     packed = nn(hidden, low[...]) + vec_ref[2:3, :1024]
     values = nn(hidden, high[:, :128]) + vec_ref[2:3, 1024:]
-    turned = packed * cos_ref[...] + swap_halves(packed) * sin_ref[...]
+    cos = jnp.concatenate([cos_ref[...]] * 8, axis=1)
+    sin = jnp.concatenate([sin_ref[...]] * 8, axis=1)
+    turned = packed * cos + swap_halves(packed) * sin
     kv[y, c, :, 0:128] = turned[:, D:].astype(BF)
     kv[y, c, :, 128:256] = values.astype(BF)
     yp, ym, y2 = up1(y), down1(y), up2(y)
@@ -1043,46 +877,129 @@
     )(*operands)
 
 
-def attention_backward_kernel(
-    g_ref, ghid2_ref, mid_ref, x_ref, vec_ref, cos_ref, sin_ref, place_ref, att_ref, qs_ref,
-    kvs_ref, probs_ref, low_ref, high_ref, m_ref,
-    gin_ref, a_out, m_out,
-    low, high, kvs, probs, m, gs, gatt, gqs, part, near, own, got, glow, ghigh, special,
-    *refs,
-):
+BACK_SLOTS = {1: 45, 0: 91}
+
+
+def backward_kernel(layer, *refs):
+    g_ref, x_ref, vec_ref, cos_ref, sin_ref, place_ref = refs[:6]
+    w_ref, hr_ref, gate_ref, up_ref, mid_ref, att_ref, qs_ref = refs[6:13]
+    kvs_ref, probs_ref, low_ref, high_ref = refs[13:17]
+    refs = refs[17:]
+    if layer == 0:
+        before, gin_ref, m_out, a_zero, a_one = refs[:5]
+        refs = refs[5:]
+    else:
+        gin_ref, m_out, a_out = refs[:3]
+        refs = refs[3:]
+    buffers, refs = refs[:7], refs[7:]
+    w, hr, gate, up, act, src, mid, att, qs = refs[:9]
+    low, high, kvs, probs, m, gatt, gqs, part, near, own, got, glow, ghigh, special = refs[9:23]
+    plane_refs, refs = refs[23:31], refs[31:]
     send_sem, recv_sem, local_sem = refs[-3:]
+    rows, back = buffers[0], buffers[1]
     spot = place()
     x, z, y, c = spot
     mail = Mail(send_sem, recv_sem)
-    loads = [
-        pltpu.make_async_copy(src, dst, local_sem.at[i])
-        for i, (src, dst) in enumerate(
-            ((m_ref, m), (high_ref, high), (probs_ref, probs), (kvs_ref, kvs), (low_ref, low))
-        )
-    ]
-    for load in loads:
+    pairs = (
+        (w_ref, w), (gate_ref, gate), (up_ref, up), (hr_ref, hr), (high_ref, high), (mid_ref, mid),
+        (att_ref, att), (probs_ref, probs), (kvs_ref, kvs), (qs_ref, qs), (low_ref, low),
+    )
+    loads = [pltpu.make_async_copy(u, v, local_sem.at[i]) for i, (u, v) in enumerate(pairs)]
+    for load in loads[:4]:
         load.start()
-    plane = PlaneSum(mail, 7, spot, m, 2, refs[:-3])
+    src[...] = g_ref[...].astype(BF)
     yp, ym, y2 = up1(y), down1(y), up2(y)
     to_yp, to_ym, other = ctx_peers(spot)
     to_y2 = device(x, z, y2, c)
     greet([to_yp, to_ym, other, to_y2] + PlaneSum.peers(spot, 3, 2))
-    loads[0].wait()
-    plane.step_one()
-    mid = mid_ref[...]
-    n, r = normal(mid)
-    ghid2 = ghid2_ref[...]
+    plane = PlaneSum(mail, 29, spot, m, 2, plane_refs)
+    older = final = None
+    if layer == 0:
+        older_mine, older_refs = refs[0], refs[1:12]
+        pair, final_refs = refs[12], refs[13:24]
+        older = AttentionSum(mail.shifted(45), spot, older_mine, before.at[1 - c], older_refs)
+        final = AttentionSum(mail.shifted(68), spot, pair.at[0], pair.at[1], final_refs)
+        older_load = pltpu.make_async_copy(before.at[c], older_mine, local_sem.at[11])
+        older_load.start()
+
+    loaded = []
+
+    def chunk(row):
+        if not loaded:
+            for load in loads[:3]:
+                load.wait()
+            loaded.append(True)
+            for load in loads[4:]:
+                load.start()
+        gz = rows[row].reshape(256, D)
+        gact = nn(gz, w[2])
+        g = gate[row].astype(F32)
+        u = up[row].astype(F32)
+        s = 1.0 / (1.0 + jnp.exp(-g))
+        silu = g * s
+        act[row] = (silu * u).astype(BF)
+        gg = (gact * u * (s + silu * (1.0 - s))).astype(BF)
+        gu = (gact * silu).astype(BF)
+        gate[row] = gg
+        up[row] = gu
+        back[row] = (nt(gg, w[0]) + nt(gu, w[1])).astype(BF).reshape(2, 128, D)
+
+    def weight_grad(member, left, right):
+        r = right[...].reshape(1024, FS)
+        for i in range(7):
+            l = left[:, :, :, 128 * i : 128 * (i + 1)].reshape(1024, 128)
+            tile = tn(l, r).astype(BF)
+            for b in range(16):
+                lo, hi = max(56 * b, 128 * i), min(56 * (b + 1), 128 * (i + 1))
+                if lo < hi:
+                    m[member, b // 4, b % 4, lo - 56 * b : hi - 56 * b] = tile[
+                        lo - 128 * i : hi - 128 * i
+                    ]
+
+    def first_filler():
+        weight_grad(2, rows, act)
+
+    def second_filler():
+        loads[3].wait()
+        weight_grad(0, hr, gate)
+
+    def third_filler():
+        weight_grad(1, hr, up)
+        plane.step_one()
+
+    def hook():
+        if older:
+            for i in range(4):
+                older.start(i)
+
+    ghid2 = mlp_exchange(
+        mail, spot, src, buffers, chunk, [first_filler, second_filler, third_filler], hook
+    )
+    if older:
+        older_load.wait()
+        older.cores()
+    for load in loads[4:7]:
+        load.wait()
+    n, r = normal(mid[...])
     t = ghid2 * vec_ref[1:2, :D]
-    gmid = g_ref[...] + r * (t - n * jnp.mean(t * n, axis=-1, keepdims=True))
+    gmid = g_ref[...].astype(F32) + r * (t - n * jnp.mean(t * n, axis=-1, keepdims=True))
     ggain_two = jnp.sum(ghid2 * n, axis=0, keepdims=True)
+    gin_ref[...] = gmid
     gy = gmid.astype(BF)
-    loads[1].wait()
     ga = nt(gy, high[:, 128:]).astype(BF)
     for h in range(H):
         gatt[h] = ga[:, HD * h : HD * (h + 1)]
-    ghigh[:, 128:] = tn(att_ref[...], gy).astype(BF)
-    loads[2].wait()
-    loads[3].wait()
+    ghigh[:, 128:] = tn(att[...], gy).astype(BF)
+    for load in loads[7:]:
+        load.wait()
+    plane.step_two()
+    for k in range(KVH):
+        heads = pl.ds(7 * k, 7)
+        gv = tn(gatt[heads].reshape(D, HD), probs[heads].reshape(D, 1024)).astype(BF)
+        for j in range(8):
+            part[j // 2, j % 2, 128 + HD * k : 128 + HD * (k + 1)] = gv[:, 128 * j : 128 * (j + 1)]
+    if older:
+        older.plane.step_two()
 
     def body(i, carry):
         for k in range(KVH):
@@ -1090,50 +1007,52 @@
             p = probs[h].astype(F32)
             gp = nt(gatt[h], kvs[2 + k])
             s = (p * (gp - jnp.sum(gp * p, axis=-1, keepdims=True))).astype(BF)
-            gs[h] = s
+            probs[h] = s
             gqs[h] = nn(s, kvs[k])
         return carry
 
     lax.fori_loop(0, 7, body, 0)
-    plane.step_two()
     for k in range(KVH):
         heads = pl.ds(7 * k, 7)
-        gk = tn(qs_ref[heads].reshape(D, HD), gs[heads].reshape(D, 1024)).astype(BF)
-        gv = tn(gatt[heads].reshape(D, HD), probs[heads].reshape(D, 1024)).astype(BF)
+        gk = tn(qs[heads].reshape(D, HD), probs[heads].reshape(D, 1024)).astype(BF)
         for j in range(8):
             part[j // 2, j % 2, HD * k : HD * (k + 1)] = gk[:, 128 * j : 128 * (j + 1)]
-            part[j // 2, j % 2, 128 + HD * k : 128 + HD * (k + 1)] = gv[:, 128 * j : 128 * (j + 1)]
-    mail.send(0, part.at[:, 1 - c], near, other)
+    mail.send(25, part.at[:, 1 - c], near, other)
+    plane.step_three()
+    cos = jnp.concatenate([cos_ref[...]] * 7, axis=1)
+    sin = jnp.concatenate([sin_ref[...]] * 7, axis=1)
     gq = jnp.concatenate([gqs[h] for h in range(H)], axis=1) * HD ** (-0.5)
-    gq = (gq * cos_ref[:, :D] - swap_halves(gq) * sin_ref[:, :D]).astype(BF)
-    inputs = x_ref[...]
+    gq = (gq * cos - swap_halves(gq) * sin).astype(BF)
+    inputs = x_ref[...].astype(F32)
     n, r = normal(inputs)
     hidden = (n * vec_ref[0:1, :D]).astype(BF)
-    mail.take(0, near, other)
+    mail.take(25, near, other)
     own[...] = (part[:, c].astype(F32) + near[...].astype(F32)).astype(BF)
-    mail.send(1, own.at[yp], got.at[0], to_yp)
-    mail.send(2, own.at[ym], got.at[1], to_ym)
-    mail.send(3, own.at[y2], got.at[2], to_y2)
+    mail.send(26, own.at[yp], got.at[0], to_yp)
+    mail.send(27, own.at[ym], got.at[1], to_ym)
+    mail.send(28, own.at[y2], got.at[2], to_y2)
+    if older:
+        older.plane.step_three()
     glow[:, :D] = tn(hidden, gq).astype(BF)
-    loads[4].wait()
     ghid = nt(gq, low[:, :D])
-    plane.step_three()
-    mail.take(1, got.at[0], to_ym)
-    mail.take(2, got.at[1], to_yp)
-    mail.take(3, got.at[2], to_y2)
+    bias_q = jnp.sum(gq.astype(F32), axis=0, keepdims=True)
+    plane.step_four()
+    mail.take(26, got.at[0], to_ym)
+    mail.take(27, got.at[1], to_yp)
+    mail.take(28, got.at[2], to_y2)
     total = own[y].astype(F32) + got[0].astype(F32) + got[1].astype(F32) + got[2].astype(F32)
     total = total.T
     gk = total[:, :128]
-    gk = (gk * cos_ref[:, D:] - swap_halves(gk) * sin_ref[:, D:]).astype(BF)
+    gk = (gk * cos_ref[...] - swap_halves(gk) * sin_ref[...]).astype(BF)
     gv = total[:, 128:].astype(BF)
     ghid = ghid + nt(gk, low[:, D:]) + nt(gv, high[:, :128])
     glow[:, D:] = tn(hidden, gk).astype(BF)
     ghigh[:, :128] = tn(hidden, gv).astype(BF)
     t = ghid * vec_ref[0:1, :D]
-    gin_ref[...] = gmid + r * (t - n * jnp.mean(t * n, axis=-1, keepdims=True))
+    gin_ref[...] += r * (t - n * jnp.mean(t * n, axis=-1, keepdims=True))
     ggain_one = jnp.sum(ghid * n, axis=0, keepdims=True)
-    plane.step_four()
-    bias_q = jnp.sum(gq.astype(F32), axis=0, keepdims=True)
+    if older:
+        older.plane.step_four()
     bias_k = jnp.sum(gk.astype(F32), axis=0, keepdims=True)
     bias_v = jnp.sum(gv.astype(F32), axis=0, keepdims=True)
     bias = jnp.concatenate([bias_q, bias_k], axis=1)
@@ -1149,32 +1068,63 @@
             + nn(place_ref[2, :, 0:16], special[...])
         ).astype(BF)
         for k in range(16):
-            ctx = k % 8
-            a_out[ctx % 2, ctx // 2, g // 2, 2 * (g % 2) + k // 8] = block[16 * k : 16 * (k + 1)]
-    plane.step_five(m_out)
+            core, line, column = k % 2, k % 8 // 2, 2 * (g % 2) + k // 8
+            piece = block[16 * k : 16 * (k + 1)]
+            if layer == 0:
+                pair[lax.rem(c + core, 2), line, g // 2, column] = piece
+            else:
+                a_out[core, line, g // 2, column] = piece
+        if layer == 0 and g % 2 == 1:
+            final.start(g // 2)
+    if layer == 0:
+        older.rows()
+        plane.step_five(m_out)
+        final.cores()
+        older.last(a_one)
+        final.plane.step_two()
+        final.plane.step_three()
+        final.plane.step_four()
+        final.rows()
+        final.last(a_zero)
+    else:
+        plane.step_five(m_out)
     mail.finish()
 
 
-def attention_backward(layer, grad_output, grad_hidden_two, kept, vectors, tables, place_rows, m_grads):
-    x, mid, att, qs, kvs, probs, low, high = kept
+def backward(layer, grad_output, x, vectors, tables, place_rows, w, kept_mlp, kept, before):
     anywhere = pl.BlockSpec(memory_space=pl.ANY)
     vmem = pl.BlockSpec(memory_space=pltpu.VMEM)
+    operands = [grad_output, x, vectors, *tables, place_rows, w, *kept_mlp, *kept]
+    out_shape = [jax.ShapeDtypeStruct((128, D), F32), jax.ShapeDtypeStruct((3, 56, FS), F32)]
+    extra = []
+    if layer == 0:
+        operands.append(before)
+        out_shape += [jax.ShapeDtypeStruct((16, 1024), F32)] * 2
+        extra = [pltpu.VMEM((4, 4, 4, 16, 1024), BF)] + AttentionSum.scratch()
+        extra += [pltpu.VMEM((2, 4, 4, 4, 16, 1024), BF)] + AttentionSum.scratch()
+    else:
+        out_shape.append(jax.ShapeDtypeStruct((2, 4, 4, 4, 16, 1024), BF))
     return pl.pallas_call(
-        attention_backward_kernel,
-        out_shape=(
-            jax.ShapeDtypeStruct((128, D), F32),
-            jax.ShapeDtypeStruct((2, 4, 4, 4, 16, 1024), BF),
-            jax.ShapeDtypeStruct((3, 56, FS), F32),
-        ),
-        in_specs=[vmem] * 10 + [anywhere] * 5,
-        out_specs=[vmem] * 3,
-        scratch_shapes=[
+        functools.partial(backward_kernel, layer),
+        out_shape=tuple(out_shape),
+        in_specs=[vmem] * 6 + [anywhere] * (len(operands) - 6),
+        out_specs=[vmem] * len(out_shape),
+        scratch_shapes=mlp_scratch()
+        + [
+            pltpu.VMEM((3, D, FS), BF),
+            pltpu.VMEM((4, 2, 128, D), BF),
+            pltpu.VMEM((4, 256, FS), BF),
+            pltpu.VMEM((4, 256, FS), BF),
+            pltpu.VMEM((4, 256, FS), BF),
+            pltpu.VMEM((128, D), BF),
+            pltpu.VMEM((128, D), F32),
+            pltpu.VMEM((128, D), BF),
+            pltpu.VMEM((H, 128, HD), BF),
             pltpu.VMEM((D, 1024), BF),
             pltpu.VMEM((D, 1024), BF),
             pltpu.VMEM((4, 1024, HD), BF),
             pltpu.VMEM((H, 128, 1024), BF),
             pltpu.VMEM((3, 4, 4, 56, FS), BF),
-            pltpu.VMEM((H, 128, 1024), BF),
             pltpu.VMEM((H, 128, HD), BF),
             pltpu.VMEM((H, 128, HD), F32),
             pltpu.VMEM((4, 2, 256, 128), BF),
@@ -1186,19 +1136,17 @@
             pltpu.VMEM((16, 1024), BF),
         ]
         + PlaneSum.scratch(3, 2, 56, FS)
+        + extra
         + [
-            pltpu.SemaphoreType.DMA((23,)),
-            pltpu.SemaphoreType.DMA((23,)),
-            pltpu.SemaphoreType.DMA((5,)),
+            pltpu.SemaphoreType.DMA((BACK_SLOTS[layer],)),
+            pltpu.SemaphoreType.DMA((BACK_SLOTS[layer],)),
+            pltpu.SemaphoreType.DMA((12,)),
         ],
         compiler_params=pltpu.CompilerParams(
-            collective_id=14 + layer, has_side_effects=True, vmem_limit_bytes=56 * 1024 * 1024
+            collective_id=14 + layer, has_side_effects=True, vmem_limit_bytes=60 * 1024 * 1024
         ),
-        name="attention_backward_%d" % layer,
-    )(
-        grad_output, grad_hidden_two, mid, x, vectors, *tables, place_rows, att, qs,
-        kvs, probs, low, high, m_grads.reshape(3, 4, 4, 56, FS),
-    )
+        name="backward_layer_%d" % layer,
+    )(*operands)
 
 
 def select_matrix():
@@ -1255,9 +1203,9 @@
     all_pos = (span_order[:, None] * span_len + offsets[None, :]).reshape(-1)
     positions = (local_pos[:, None], all_pos[None, :])
     frequency = rope_base ** (-jnp.arange(HD // 2, dtype=F32) * 2.0 / HD)
-    angles = local_pos.astype(F32)[:, None] * frequency[None, :]
-    cosine, sine = jnp.cos(angles), jnp.sin(angles)
-    tables = (jnp.tile(cosine, (1, 32)), jnp.tile(jnp.concatenate([-sine, sine], axis=1), (1, 16)))
+    angles = local_pos.astype(F32)[:, None] * jnp.tile(frequency, 4)[None, :]
+    sign = jnp.tile(jnp.concatenate([-jnp.ones(32, F32), jnp.ones(32, F32)]), 2)
+    tables = (jnp.cos(angles), jnp.sin(angles) * sign[None, :])
     chosen = select_matrix()
     pick = jnp.asarray(np.concatenate([chosen, np.zeros((14, 256), np.float32)]), BF)
     spread = np.zeros((3, 256, 112), np.float32)
@@ -1266,7 +1214,7 @@
 
     m_block = jnp.stack([w_gate, w_up, w_down.transpose(0, 2, 1)], axis=1)
     a_zero, row_one, m_x, m_z = first_gather(gain_one, w_qkv, b_qkv, w_out, gain_two, m_block)
-    state_zero = tokens.reshape(local_len, width).astype(F32)
+    state_zero = tokens.reshape(local_len, width)
     state_one, *saved_zero, m_zero, m_one, a_one = forward(
         0, state_zero, a_zero, m_x, pick, tables, positions, row_one, m_block, m_z
     )
@@ -1274,22 +1222,20 @@
     state, *saved_one = forward(1, state_one, a_one, m_full[1], pick, tables, positions)
     vectors = (saved_zero[0], saved_one[0])
     kept_layers = [
-        ((state_zero,) + tuple(saved_zero[1:8]), saved_zero[8:]),
-        ((state_one,) + tuple(saved_one[1:8]), saved_one[8:]),
+        (saved_zero[1:8], saved_zero[8:]),
+        (saved_one[1:8], saved_one[8:]),
     ]
-    grad_state = cotangent.reshape(local_len, width).astype(F32)
-    a_grads = None
-    sums = [None, None]
-    a_sums = [None, None]
-    for l in reversed(range(LAYERS)):
-        kept, kept_mlp = kept_layers[l]
-        grad_hidden_two, m_grads, *older = mlp_backward(l, grad_state, m_full[l], *kept_mlp, a_grads)
-        if older:
-            a_sums[l + 1] = older[0]
-        grad_state, a_grads, sums[l] = attention_backward(
-            l, grad_state, grad_hidden_two, kept, vectors[l], tables, spread, m_grads
-        )
-    a_sums[0] = last_sum(a_grads)
+    grad_one = cotangent.reshape(local_len, width)
+    (state_in, kept, kept_mlp) = (state_one,) + kept_layers[1]
+    grad_zero, m_sum_one, a_grads = backward(
+        1, grad_one, state_in, vectors[1], tables, spread, m_full[1], kept_mlp, kept, None
+    )
+    kept, kept_mlp = kept_layers[0]
+    grad_state, m_sum_zero, a_sum_zero, a_sum_one = backward(
+        0, grad_zero, state_zero, vectors[0], tables, spread, m_full[0], kept_mlp, kept, a_grads
+    )
+    a_sums = (a_sum_zero, a_sum_one)
+    sums = (m_sum_zero, m_sum_one)
     stacks = tuple(assemble(a_sums, sums)) + (jnp.stack([sums[0][2].T, sums[1][2].T]),)
     output = state.astype(BF).reshape(sequences, local_len, width)
     input_grad = grad_state.reshape(sequences, local_len, width)

time: 367 us -> 342 us (0.932)
  Pallas kernels: 331 us -> 313 us
  local copies, waits for them, and re-layouts: 23.4 us -> 16.1 us
    pallas_call x5 -> x2, Pallas kernels: 177 us -> 159 us  [backward(): pl.pallas_call(functools.partial(backward_kernel, layer), out_shape=tuple...]
    unnamed x42 -> x24, local copies, waits for them, and re-layouts: 18.7 us -> 12.7 us
where the time goes in v2:
time: 342 us; the launch traced here: 336 us
  Pallas kernels  313 us (92%)
  local copies, waits for them, and re-layouts  16.1 us (5%)
  other arithmetic  6.11 us (2%)
    pallas_call x2, Pallas kernels, backward(): pl.pallas_call(functools.partial(backward_kernel, layer), out_shape=tuple...  159 us
    pallas_call x2, Pallas kernels, forward(): pl.pallas_call(functools.partial(forward_kernel, layer), out_shape=tuple(...  117 us
    pallas_call x1, Pallas kernels, first_gather(): pl.pallas_call(first_gather_kernel, out_shape=(jax.ShapeDtypeStruct((2, 4...  34.5 us
    unnamed x24, local copies, waits for them, and re-layouts  12.7 us

profile of v2, /device:TPU:0, one launch (start us, length us, event | category | flops | bytes accessed | tf_op | source)
XLA Modules:
  0.0 336.2 jit_solution(3599774946295658240)
XLA Ops:
  0.6 0.7 dynamic-slice_multiply_fusion
  1.4 0.7 broadcast_multiply_fusion
  2.0 0.7 tile.5
  2.7 0.1 mul.41
  2.8 0.1 mul.38
  2.9 0.1 iota_add_fusion.1
  3.0 0.1 convert_element_type.14
  3.0 0.1 iota_add_fusion
  3.1 0.7 add.62.refs_7_
  3.8 0.7 copy.25.out_ref
  4.5 0.8 copy.24.qkv_ref
  5.3 0.8 add.63.refs_6_
  6.1 1.0 fusion
  7.0 1.1 pad_maximum_fusion.m_ref.refs_9_
  8.1 0.0 copy-start.5
  8.2 0.6 copy-done.5
  8.8 0.0 copy-start.6
  8.8 0.7 copy-done.6
  9.5 0.0 copy-start.7
  9.5 0.7 copy-done.7
  10.1 0.0 copy-start.1
  10.1 34.5 %first_gather.1 = (bf16[2,4,4,4,16,1024]{5,4,3,2,1,0:T(8,128)(2,1)S(1)}, bf16[4,16,1024]{2,1,0:T(8,128)(2,1)S(1)}, bf16[2,4,56,608]{3,2,1,0:T(8,128)(2,1)S(1)}, bf16[1,4,56,608]{3,2,1,0:T(8,128)(2,1)S(1)}) custom-call(bf16[2,7]{1,0:T(2,128)(2,1)S(1)} %copy-done.5, bf16[2,7,1152]{2,1,0:T(8,128)(2,1)S(1)} %copy.24.qkv_ref, bf16[2,9]{1,0:T(2,128)(2,1)S(1)} %copy-done.6, ...), custom_call_target="tpu_custom_call" | custom-call | tf_op jit(solution)/shard_map/first_gather/pallas_call | solution.py:309
  44.7 0.0 copy-start
  44.7 2.0 copy-done
  46.7 0.0 copy-start.2
  46.7 0.8 copy-done.2
  47.5 0.0 copy-start.3
  47.5 0.7 copy-done.3
  48.2 0.0 copy-start.4
  48.2 0.7 copy-done.4
  48.9 0.0 copy-done.1
  48.9 66.3 %forward_layer_0.1 = (f32[128,896]{1,0:T(8,128)}, f32[8,1152]{1,0:T(8,128)}, f32[128,896]{1,0:T(8,128)}, bf16[128,896]{1,0:T(8,128)(2,1)}, bf16[14,128,64]{2,1,0...) custom-call(bf16[128,896]{1,0:T(8,128)(2,1)} %bitcast.27, ...), custom_call_target="tpu_custom_call" | custom-call | tf_op jit(solution)/shard_map/forward_layer_0/pallas_call | solution.py:844
  115.3 50.4 %forward_layer_1.1 = (f32[128,896]{1,0:T(8,128)}, f32[8,1152]{1,0:T(8,128)}, f32[128,896]{1,0:T(8,128)}, bf16[128,896]{1,0:T(8,128)(2,1)}, bf16[14,128,64]{2,1,0...) custom-call(f32[128,896]{1,0:T(8,128)} %get-tuple-element.61.refs_0_, ...), custom_call_target="tpu_custom_call" | custom-call | tf_op jit(solution)/shard_map/forward_layer_1/pallas_call | solution.py:844
  165.7 1.7 convert_bitcast_fusion
  167.4 62.3 %backward_layer_1.1 = (f32[128,896]{1,0:T(8,128)}, f32[3,56,608]{2,1,0:T(8,128)}, bf16[2,4,4,4,16,1024]{5,4,3,2,1,0:T(8,128)(2,1)}) custom-call(bf16[128,896]{1,0:T(8,128)(2,1)} %bitcast.30, f32[128,896]{1,0:T(8,128)} %get-tuple-element.61.refs_0_.refs_1_, f32[8,1152]{1,0:T(8,128)} %get-tuple-element.65.refs_2_, ...), custom_call_target="tpu_custom_call" | custom-call | tf_op jit(solution)/shard_map/backward_layer_1/pallas_call | solution.py:1107
  229.7 97.1 %backward_layer_0.1 = (f32[128,896]{1,0:T(8,128)}, f32[3,56,608]{2,1,0:T(8,128)}, f32[16,1024]{1,0:T(8,128)}, f32[16,1024]{1,0:T(8,128)}) custom-call(f32[128,896]{1,0:T(8,128)} %get-tuple-element.76.refs_0_, bf16[128,896]{1,0:T(8,128)(2,1)} %bitcast.28, f32[8,1152]{1,0:T(8,128)} %get-tuple-element.77.refs_2_, ...), custom_call_target="tpu_custom_call" | custom-call | tf_op jit(solution)/shard_map/backward_layer_0/pallas_call | solution.py:1107
  326.8 0.0 copy-start.8
  326.8 1.1 slice_bitcast_fusion
  327.9 2.1 assemble.1
  330.0 0.7 pad_maximum_fusion.1
  330.7 1.3 copy.29
  332.0 1.5 copy.30
  333.5 1.5 copy.28
  335.0 0.0 copy-done.8
  335.0 0.8 copy.32
  (2 shorter events, 0.0 us)
Async XLA Ops:
  8.1 0.7 copy-start.5
  8.8 0.7 copy-start.6
  9.5 0.7 copy-start.7
  10.1 38.8 %copy-start.1 = (bf16[2,3,56,608]{3,2,1,0:T(8,128)(2,1)}, bf16[2,3,56,608]{3,2,1,0:T(8,128)(2,1)S(1)}, u32[]{:S(2)}) copy-start(bf16[2,3,56,608]{3,2,1,0:T(8,128)(2,1)S(1)} %pad_maximum_fusion.m_ref.refs_9_) | copy-start | bytes 1225732
  44.7 2.0 copy-start
  46.7 0.8 copy-start.2
  47.5 0.7 copy-start.3
  48.2 0.7 copy-start.4
  326.8 8.2 %copy-start.8 = (f32[128,896]{1,0:T(8,128)S(1)}, f32[128,896]{1,0:T(8,128)}, u32[]{:S(2)}) copy-start(f32[128,896]{1,0:T(8,128)} %get-tuple-element.90) | copy-start | bytes 1376260
